TPU v7x, 256 devices: a whole 4x4x8 slice. The times are simulated.
256 devices in a mesh: dp: 4 (over x_lo, core), seq: 32 (over z, y), mp: 2 (over x_hi).
Axes of the slice: x: 4 (x_hi: 2, x_lo: 2; x = x_hi * 2 + x_lo), y: 4, z: 8, core: 2. Of those that a mesh axis runs over, the one named last changes fastest.
Arguments:
- queries: bfloat16 [4, 4096, 2048], P('dp', 'seq', 'mp'), may hold values from -6 to 6
- keys: bfloat16 [4, 4096, 2048], P('dp', 'seq', 'mp'), may hold values from -6 to 6
- values: bfloat16 [4, 4096, 2048], P('dp', 'seq', 'mp'), may hold values from -6 to 6
- cross_queries: bfloat16 [4, 4096, 2048], P('dp', 'seq', 'mp'), may hold values from -6 to 6
- neighbour_ids: int32 [4, 64, 2, 2], P('dp', 'seq'), may hold values from 0 to 5, as said below
- database: bfloat16 [4, 2, 6, 128, 2048], P('dp', None, None, None, 'mp'), may hold values from -6 to 6
- out_weight: bfloat16 [2048, 4096], P('mp'), may hold values from -2.5 to 2.5
Outputs:
- mixed: bfloat16 [4, 4096, 4096], P('dp', 'seq', 'mp')
Inputs may be any that keep to these rules, and one draw needn't show every extreme that they name: `neighbour_ids`: entry [b, c, n, 0] is the database shard and [b, c, n, 1] the block of the n-th neighbour of span c of sequence b. Among the neighbours of the 2 spans held by one index of dp and seq, at most 3 name one shard; in every draw, for some seq index, the spans of every dp index name exactly 3 neighbours of one common shard.
All inputs are finite; a program needn't handle non-finite values.
Results may differ from a plain program's by a relative error of at most 0.012.
Values may be sent and summed in bfloat16 or wider, within the bound.
No kernel may reach another device: no remote copies, remote signals or barrier semaphores. Data moves between devices by JAX's collectives and lax.ppermute only.
A program may use at most 128 MiB of HBM per device.

v0:
```python
import functools
import math

import jax
import jax.numpy as jnp
from jax import lax
from jax.experimental import pallas as pl
from jax.experimental.pallas import tpu as pltpu
from jax.sharding import Mesh, PartitionSpec as P

HD = 128
ROWS = 128
HEADS = 8
ZS, YS = 8, 4
RETR = 128
STAT = 32
LOW = -1e30
EXP2_SCALE = math.log2(math.e) / math.sqrt(HD)
VMEM_LIMIT = 24 * 1024 * 1024

VMEM = pl.BlockSpec(memory_space=pltpu.VMEM)
SMEM = pl.BlockSpec(memory_space=pltpu.SMEM)
F32 = jnp.float32
BF16 = jnp.bfloat16


def params(limit=VMEM_LIMIT):
    return pltpu.CompilerParams(vmem_limit_bytes=limit)


def flipped(block):
    return jnp.transpose(block.astype(F32)).astype(BF16)


def split_kernel(q_ref, k_ref, v_ref, out_ref):
    for h in range(HEADS):
        cols = pl.ds(h * HD, HD)
        out_ref[h, 0] = k_ref[:, cols]
        out_ref[h, 1] = flipped(v_ref[:, cols])
        out_ref[h, 2] = flipped(q_ref[:, cols])


def split_heads(queries, keys, values):
    return pl.pallas_call(
        split_kernel,
        out_shape=jax.ShapeDtypeStruct((HEADS, 3, ROWS, HD), BF16),
        in_specs=[VMEM] * 3,
        out_specs=VMEM,
        compiler_params=params(56 * 1024 * 1024),
        name="split_heads",
        cost_estimate=pl.CostEstimate(flops=0, bytes_accessed=1536 * 1024, transcendentals=0),
    )(queries, keys, values)


def shade_of(y, step):
    return jnp.where(lax.rem(y + step, YS) < y, 0.0, LOW).astype(F32)


def fold(state, scores, v_tile):
    row_max, total, summed = state
    new_max = jnp.maximum(row_max, jnp.max(scores, axis=0, keepdims=True))
    weights = jnp.exp2((scores - new_max) * EXP2_SCALE)
    fade = jnp.exp2((row_max - new_max) * EXP2_SCALE)
    total = total * fade + jnp.sum(weights, axis=0, keepdims=True)
    summed = summed * fade + jnp.dot(v_tile, weights.astype(BF16), preferred_element_type=F32)
    return new_max, total, summed


def attend_kernel(steps, count, first, last, y_ref, own_ref, *refs):
    part_refs, refs = refs[:count], refs[count:]
    if not first:
        old_refs, refs = refs[:3], refs[3:]
    wide, results = refs[-1], refs[:-1]
    y = y_ref[0]
    left = lax.broadcasted_iota(jnp.int32, (1, 2 * ROWS), 1) < ROWS
    key_pos = lax.broadcasted_iota(jnp.int32, (ROWS, 2 * ROWS), 0)
    query_pos = lax.broadcasted_iota(jnp.int32, (ROWS, 2 * ROWS), 1)
    halves = count // len(steps)

    def block(part, z, kind):
        depth = ZS // halves
        return part_refs[part * halves + z // depth][z % depth, kind]

    for pair in range(ZS // 2):
        low, high = 2 * pair, 2 * pair + 1
        wide[:, 0:ROWS] = own_ref[low, 2]
        wide[:, ROWS:] = own_ref[high, 2]
        places = [(part, z) for part in range(len(steps)) for z in range(high + 1)]
        k_tile = jnp.concatenate([block(part, z, 0) for part, z in places], axis=0)
        v_tile = jnp.concatenate([block(part, z, 1) for part, z in places], axis=1)
        scores = jnp.dot(k_tile, wide[...], preferred_element_type=F32)
        pieces = []
        for part, step in enumerate(steps):
            start = part * (high + 1) * ROWS
            middle, end = start + low * ROWS, start + high * ROWS
            if step == 0:
                same_z = jnp.where(left & (key_pos > query_pos), LOW, 0.0)
                next_z = jnp.where(left | (key_pos > query_pos - ROWS), LOW, 0.0)
            else:
                shade = shade_of(y, step)
                same_z, next_z = jnp.where(left, shade, 0.0), jnp.where(left, LOW, shade)
            if low:
                pieces.append(scores[start:middle])
            pieces.append(scores[middle:end] + same_z)
            pieces.append(scores[end : end + ROWS] + next_z)
        scores = jnp.concatenate(pieces, axis=0)
        if first:
            row_max = jnp.max(scores, axis=0, keepdims=True)
            weights = jnp.exp2((scores - row_max) * EXP2_SCALE)
            total = jnp.sum(weights, axis=0, keepdims=True)
            summed = jnp.dot(v_tile, weights.astype(BF16), preferred_element_type=F32)
        else:
            old = [
                jnp.concatenate([ref[z : z + 1, :] for z in (low, high)], axis=1)
                for ref in old_refs[:2]
            ] + [jnp.concatenate([old_refs[2][z] for z in (low, high)], axis=1)]
            row_max, total, summed = fold(old, scores, v_tile)
        for z, side in ((low, slice(0, ROWS)), (high, slice(ROWS, None))):
            if last:
                results[0][z] = (summed[:, side] * (1.0 / total[:, side])).astype(BF16)
            else:
                results[0][z : z + 1, :] = row_max[:, side]
                results[1][z : z + 1, :] = total[:, side]
                results[2][z] = summed[:, side]


def attend(y_index, own, steps, parts, state=(), last=False):
    rows = jax.ShapeDtypeStruct((ZS, ROWS), F32)
    kept = (rows, rows, jax.ShapeDtypeStruct((ZS, HD, ROWS), F32))
    share = len(steps)
    return pl.pallas_call(
        functools.partial(attend_kernel, steps, len(parts), not state, last),
        out_shape=jax.ShapeDtypeStruct((ZS, HD, ROWS), BF16) if last else kept,
        in_specs=[SMEM] + [VMEM] * (1 + len(parts) + len(state)),
        out_specs=VMEM if last else (VMEM,) * 3,
        scratch_shapes=[pltpu.VMEM((HD, 2 * ROWS), BF16)],
        compiler_params=params(),
        name="attend_far" if last else "attend_near",
        cost_estimate=pl.CostEstimate(
            flops=350_000_000 * share, bytes_accessed=1_500_000, transcendentals=650_000 * share
        ),
    )(y_index, own, *parts, *state)


def cross_kernel(ids0_ref, ids1_ref, place_ref, q0_ref, q1_ref, db_ref, out0_ref, out1_ref, *refs):
    top, total, summed, blocks, queries, arrived, ready = refs
    here = place_ref[0]
    fetches = [
        pltpu.make_async_copy(q_ref, queries.at[slot], arrived.at[slot])
        for slot, q_ref in enumerate((q0_ref, q1_ref))
    ]
    for fetch in fetches:
        fetch.start()

    def named(ids_ref, index):
        which, span, n = (index + 2) // 4, lax.rem(index // 2 + 1, 2), lax.rem(index, 2)
        return ids_ref[which, span, n, 0], ids_ref[which, span, n, 1]

    def fetch_block(block, place):
        return pltpu.make_async_copy(db_ref.at[:, block], blocks.at[place], ready.at[place])

    for slot, ids_ref in enumerate((ids0_ref, ids1_ref)):

        def request(index, carry, slot=slot, ids_ref=ids_ref):
            shard, block = named(ids_ref, index)

            @pl.when(shard == here)
            def _():
                fetch_block(block, 6 * slot + index).start()

            return carry

        lax.fori_loop(0, 6, request, 0)
    for fetch in fetches:
        fetch.wait()
    row = lax.broadcasted_iota(jnp.int32, (1, ROWS), 1)
    group_of = (row + 1) // 64
    for slot, ids_ref, out_ref in ((0, ids0_ref, out0_ref), (1, ids1_ref, out1_ref)):
        top[...] = jnp.full(top.shape, LOW, F32)
        total[...] = jnp.zeros(total.shape, F32)
        summed[...] = jnp.zeros(summed.shape, F32)

        def neighbour(index, carry, ids_ref=ids_ref, slot=slot):
            shard, block = named(ids_ref, index)
            place = 6 * slot + index

            @pl.when(shard == here)
            def _():
                fetch_block(block, place).wait()
                inside = group_of == index // 2
                cols = [slice(h * HD, (h + 1) * HD) for h in range(HEADS)]
                scores = [
                    lax.dot_general(
                        blocks[place, 0, :, c],
                        queries[slot, :, c],
                        (((1,), (1,)), ((), ())),
                        preferred_element_type=F32,
                    )
                    for c in cols
                ]
                old_max = top[...]
                new_max = jnp.concatenate(
                    [jnp.max(block_scores, axis=0, keepdims=True) for block_scores in scores], axis=0
                )
                new_max = jnp.where(inside, jnp.maximum(old_max, new_max), old_max)
                fade = jnp.exp2((old_max - new_max) * EXP2_SCALE)
                weights = [
                    jnp.where(
                        inside, jnp.exp2((scores[h] - new_max[h : h + 1]) * EXP2_SCALE), 0.0
                    )
                    for h in range(HEADS)
                ]
                sums = [jnp.sum(w, axis=0, keepdims=True) for w in weights]
                products = [
                    lax.dot_general(
                        blocks[place, 1, :, cols[h]],
                        weights[h].astype(BF16),
                        (((0,), (0,)), ((), ())),
                        preferred_element_type=F32,
                    )
                    for h in range(HEADS)
                ]
                top[...] = new_max
                total[...] = total[...] * fade + jnp.concatenate(sums, axis=0)
                for h in range(HEADS):
                    summed[h] = summed[h] * fade[h : h + 1] + products[h]

            return carry

        lax.fori_loop(0, 6, neighbour, 0)
        sums = total[...]
        some = sums > 0.0
        safe = jnp.where(some, sums, 1.0)
        inverse = 1.0 / safe
        for h in range(HEADS):
            out_ref[h * HD : (h + 1) * HD, :] = (summed[h] * inverse[h : h + 1, :]).astype(BF16)
        level = jnp.where(some, top[...] * EXP2_SCALE + jnp.log2(safe), LOW)
        high = level.astype(BF16).astype(F32)
        middle = (level - high).astype(BF16).astype(F32)
        low = level - high - middle
        stats = jnp.concatenate([high, middle, low, jnp.zeros_like(low)], axis=0)
        out_ref[HEADS * HD :, :] = stats.astype(BF16)


def cross_attend(place, ids, queries, database):
    shape = jax.ShapeDtypeStruct((HEADS * HD + STAT, ROWS), BF16)
    return pl.pallas_call(
        cross_kernel,
        out_shape=(shape,) * 2,
        in_specs=[SMEM] * 3 + [pl.BlockSpec(memory_space=pl.ANY)] * 3,
        out_specs=(VMEM,) * 2,
        scratch_shapes=[
            pltpu.VMEM((HEADS, ROWS), F32),
            pltpu.VMEM((HEADS, ROWS), F32),
            pltpu.VMEM((HEADS, HD, ROWS), F32),
            pltpu.VMEM((12, 2, RETR, HEADS * HD), BF16),
            pltpu.VMEM((2, ROWS, HEADS * HD), BF16),
            pltpu.SemaphoreType.DMA((2,)),
            pltpu.SemaphoreType.DMA((12,)),
        ],
        compiler_params=params(56 * 1024 * 1024),
        name="cross_attend",
        cost_estimate=pl.CostEstimate(
            flops=2_000_000_000, bytes_accessed=5_000_000, transcendentals=1_000_000
        ),
    )(*ids, place, *queries, database)


COLS = 2048


def join_kernel(place_ref, self_ref, *refs):
    part_refs, att_ref = refs[0:4], refs[4]
    row = lax.broadcasted_iota(jnp.int32, (1, ROWS), 1)
    live = jnp.where((row >= 63) | (place_ref[0] > 0), 1.0, 0.0).astype(F32)
    levels = []
    for part in part_refs:
        stats = part[HEADS * HD :, :].astype(F32)
        levels.append(stats[0:8] + stats[8:16] + stats[16:24])
    top = functools.reduce(jnp.maximum, levels)
    shares = [jnp.exp2(level - top) for level in levels]
    whole = functools.reduce(jnp.add, shares)
    shares = [share / whole * live for share in shares]
    for h in range(HEADS):
        cols = slice(h * HD, (h + 1) * HD)
        joined = self_ref[h].astype(F32)
        for part, share in zip(part_refs, shares):
            joined = joined + part[cols, :].astype(F32) * share[h : h + 1, :]
        att_ref[:, cols] = jnp.transpose(joined).astype(BF16)


def join(place, self_parts, cross_parts):
    return pl.pallas_call(
        join_kernel,
        out_shape=jax.ShapeDtypeStruct((ROWS, HEADS * HD), BF16),
        in_specs=[SMEM] + [VMEM] * 5,
        out_specs=VMEM,
        compiler_params=params(),
        name="join",
        cost_estimate=pl.CostEstimate(flops=0, bytes_accessed=1_500_000, transcendentals=4096),
    )(place, self_parts, *cross_parts)


PIECES = 4


def add_kernel(kept_ref, received_ref, out_ref, buffer, done):
    wide = COLS // PIECES
    copies = []
    for piece in range(PIECES):
        cols = slice(piece * wide, (piece + 1) * wide)
        buffer[:, cols] = (kept_ref[:, cols].astype(F32) + received_ref[:, cols].astype(F32)).astype(
            BF16
        )
        copies.append(
            pltpu.make_async_copy(buffer.at[:, cols], out_ref.at[:, cols], done.at[piece])
        )
        copies[-1].start()
    for copy in copies:
        copy.wait()


def add(kept, received):
    return pl.pallas_call(
        add_kernel,
        out_shape=jax.ShapeDtypeStruct((ROWS, COLS), BF16),
        in_specs=[VMEM] * 2,
        out_specs=pl.BlockSpec(memory_space=pl.ANY),
        scratch_shapes=[pltpu.VMEM((ROWS, COLS), BF16), pltpu.SemaphoreType.DMA((PIECES,))],
        compiler_params=params(),
        name="add",
        cost_estimate=pl.CostEstimate(flops=0, bytes_accessed=1_500_000, transcendentals=0),
    )(kept, received)


def ring(axis, step):
    count = lax.axis_size(axis)
    return [(i, (i + step) % count) for i in range(count)]


def per_device(queries, keys, values, cross_queries, neighbour_ids, database, out_weight):
    dp = ("xl", "core")
    seq = ("z", "y")
    seq_index = lax.axis_index(seq).astype(jnp.int32).reshape(1)
    y_index = lax.axis_index("y").astype(jnp.int32).reshape(1)
    place_dp = lax.axis_index(dp).astype(jnp.int32).reshape(1)
    across, beside = ring("xl", 1), ring("core", 1)
    up, down = ring("y", 1), ring("y", -1)

    earlier_ids = lax.ppermute(neighbour_ids, seq, [(i, i + 1) for i in range(ZS * YS - 1)])
    own = split_heads(queries[0], keys[0], values[0])
    own, earlier_ids = lax.optimization_barrier((own, earlier_ids))
    own = lax.all_to_all(own, "z", 0, 0, tiled=True)

    mine = cross_queries[0]
    ids = jnp.concatenate([earlier_ids, neighbour_ids], axis=0)
    from_across = lax.ppermute(mine, "xl", across)
    from_beside = lax.ppermute(mine, "core", beside)
    ids_across = lax.ppermute(ids, "xl", across)
    ids_beside = lax.ppermute(ids, "core", beside)
    own_part, beside_part = cross_attend(
        place_dp, (ids, ids_beside), (mine, from_beside), database[0]
    )
    from_across, ids_across, _ = lax.optimization_barrier((from_across, ids_across, own_part))
    from_diagonal = lax.ppermute(from_across, "core", beside)
    ids_diagonal = lax.ppermute(ids_across, "core", beside)
    across_part, diagonal_part = cross_attend(
        place_dp, (ids_across, ids_diagonal), (from_across, from_diagonal), database[0]
    )
    own, across_part, diagonal_part, beside_part = lax.optimization_barrier(
        (own, across_part, diagonal_part, beside_part)
    )

    kv = own[:, :2]
    below = lax.ppermute(kv, "y", up)
    above = lax.ppermute(kv, "y", down)
    beside_part = lax.ppermute(beside_part, "core", beside)
    across_part = lax.ppermute(across_part, "xl", across)
    diagonal_part = lax.ppermute(diagonal_part, dp, [(i, 3 - i) for i in range(4)])
    state = attend(y_index, own, (0,), (own,))
    below, above, state = lax.optimization_barrier((below, above, state))

    far_low = lax.ppermute(below[: ZS // 2], "y", up)
    far_high = lax.ppermute(above[ZS // 2 :], "y", down)
    state = attend(y_index, own, (YS - 1, 1), (below, above), state)
    far_low, far_high, state, beside_part, across_part, diagonal_part = lax.optimization_barrier(
        (far_low, far_high, state, beside_part, across_part, diagonal_part)
    )

    self_t = attend(y_index, own, (2,), (far_low, far_high), state, last=True)
    self_t = lax.all_to_all(self_t, "z", 0, 0, tiled=True)

    attended = join(seq_index, self_t, (own_part, beside_part, across_part, diagonal_part))
    xh = lax.axis_index("xh")

    def projected(half):
        columns = lax.dynamic_slice_in_dim(out_weight, half * COLS, COLS, axis=1)
        return jnp.dot(attended, columns, preferred_element_type=F32).astype(BF16)

    received = lax.ppermute(projected(1 - xh), "xh", ring("xh", 1))
    return add(projected(xh), received)[None]


def solution(mesh):
    split = Mesh(mesh.devices.reshape(2, 2, ZS, YS, 2), ("xl", "core", "z", "y", "xh"))
    dp, seq = ("xl", "core"), ("z", "y")
    placed = (
        P(dp, seq, "xh"),
        P(dp, seq, "xh"),
        P(dp, seq, "xh"),
        P(dp, seq, "xh"),
        P(dp, seq, None, None),
        P(dp, None, None, None, "xh"),
        P("xh", None),
    )
    return jax.shard_map(
        per_device, mesh=split, in_specs=placed, out_specs=P(dp, seq, "xh"), check_vma=False
    )
```

profile of v0, /device:TPU:2, one launch (start us, length us, event | category | flops | bytes accessed | tf_op | source)
XLA Modules:
  0.0 104.1 jit_solution(2306033435432010616)
XLA Ops:
  0.0 3.5 %collective-permute-start = (s32[1,2,2,2]{3,2,1,0:T(2,128)}, s32[1,2,2,2]{3,2,1,0:T(2,128)S(1)}, u32[]{:S(2)}, u32[]{:S(2)}) collective-permute-start(s32[1,2,2,2]{3,2,1,0:T(2,128)} %param.11), channel_id=1, source_target_pairs={{0,2},{2,4},{4,6},{6,8},{8,10},{10,12},{12,14},{14,16},{16,18},{18... | collective-permute-start | bytes 104 | tf_op jit(solution)/shard_map/ppermute | solution.py:350
  3.5 2.2 %split_heads.1 = bf16[8,3,128,128]{3,2,1,0:T(8,128)(2,1)} custom-call(bf16[128,1024]{1,0:T(8,128)(2,1)} %bitcast.11, bf16[128,1024]{1,0:T(8,128)(2,1)} %bitcast.12, bf16[128,1024]{1,0:T(8,128)(2,1)} %bitcast.13), custom_call_target="tpu_custom_call" | custom-call | bytes 1572864 | tf_op jit(solution)/shard_map/split_heads/pallas_call | solution.py:44
  5.7 0.0 collective-permute-done
  5.7 11.8 %all-to-all-start = ((bf16[8,3,128,128]{3,2,1,0:T(8,128)(2,1)}), bf16[8,3,128,128]{3,2,1,0:T(8,128)(2,1)S(1)}, u32[]{:S(2)}, u32[]{:S(2)}) async-start(bf16[8,3,128,128]{3,2,1,0:T(8,128)(2,1)} %split_heads.1), calls=%async_computation | async-start | bytes 1572864 | tf_op jit(solution)/shard_map/all_to_all | solution.py:353
  17.5 0.0 collective-permute-start.4
  17.5 0.6 collective-permute-start.1
  18.1 0.7 constant_dynamic-update-slice_fusion.ids0_ref
  18.8 0.1 collective-permute-start.3
  18.9 1.5 %collective-permute-start.2 = (s32[2,2,2,2]{3,2,1,0:T(2,128)S(1)}, s32[2,2,2,2]{3,2,1,0:T(2,128)S(1)}, u32[]{:S(2)}, u32[]{:S(2)}) collective-permute-start(s32[2,2,2,2]{3,2,1,0:T(2,128)S(1)} %constant_dynamic-update-slice_fusion.ids0_ref), channel_id=1, source_target_pairs={{0,128},{128,0},{1,129},{129,1},{2,130},{130,2},{3,131},{131,3},{4... | collective-permute-start | bytes 200 | tf_op jit(solution)/shard_map/ppermute | solution.py:359
  20.4 0.0 collective-permute-done.3.ids1_ref
  20.5 0.0 collective-permute-done.4.q1_ref
  20.5 0.6 copy-done.6
  21.0 0.1 copy-done.3
  21.2 4.4 %cross_attend.2 = (bf16[1056,128]{1,0:T(8,128)(2,1)}, bf16[1056,128]{1,0:T(8,128)(2,1)}) custom-call(s32[2,2,2,2]{3,2,1,0:T(2,128)} %copy-done.1, s32[2,2,2,2]{3,2,1,0:T(2,128)} %copy-done.6, s32[1]{0:T(128)} %bitcast.6.place_ref, bf16[128,1024]{1,0:T(8,128)(2,1)} %bitcast.18, bf16[128,1024]{1,0:T(8,128)(2,1)} %copy-done.3, bf16[2,6,128,1024]{3,2,1,0:T(8,128)(2,1)} %bitcast.14), custom_call_target="tpu_custom_call" | custom-call | flops 2000000000 | bytes 5000000 | tf_op jit(solution)/shard_map/cross_attend/pallas_call | solution.py:247
  25.6 0.0 copy-start
  25.6 0.9 collective-permute-done.2.ids0_ref
  26.5 0.0 collective-permute-done.1.q0_ref
  26.5 0.1 collective-permute-start.6
  26.6 0.5 collective-permute-start.5
  27.1 1.0 collective-permute-done.5.ids1_ref
  28.1 0.0 collective-permute-done.6.q1_ref
  28.2 0.6 copy-done.7
  28.7 0.7 copy-done.4
  29.4 3.2 %cross_attend.3 = (bf16[1056,128]{1,0:T(8,128)(2,1)}, bf16[1056,128]{1,0:T(8,128)(2,1)}) custom-call(s32[2,2,2,2]{3,2,1,0:T(2,128)} %copy-done.5, s32[2,2,2,2]{3,2,1,0:T(2,128)} %copy-done.7, s32[1]{0:T(128)} %bitcast.6.place_ref, bf16[128,1024]{1,0:T(8,128)(2,1)} %copy-done.2, bf16[128,1024]{1,0:T(8,128)(2,1)} %copy-done.4, bf16[2,6,128,1024]{3,2,1,0:T(8,128)(2,1)} %bitcast.15), custom_call_target="tpu_custom_call" | custom-call | flops 2000000000 | bytes 5000000 | tf_op jit(solution)/shard_map/cross_attend/pallas_call | solution.py:247
  32.6 6.8 %all-to-all-done.own_ref.refs_0_ = bf16[8,3,128,128]{3,2,1,0:T(8,128)(2,1)S(1)} async-done(((bf16[8,3,128,128]{3,2,1,0:T(8,128)(2,1)}), bf16[8,3,128,128]{3,2,1,0:T(8,128)(2,1)S(1)}, u32[]{:S(2)}, u32[]{:S(2)}) %all-to-all-start) | async-done | bytes 786464 | tf_op jit(solution)/shard_map/all_to_all | solution.py:353
  39.5 0.1 collective-permute-start.7
  39.6 3.2 %collective-permute-start.8 = (bf16[8,2,128,128]{3,2,1,0:T(8,128)(2,1)S(1)}, bf16[8,2,128,128]{3,2,1,0:T(8,128)(2,1)S(1)}, u32[]{:S(2)}, u32[]{:S(2)}) collective-permute-start(bf16[8,2,128,128]{3,2,1,0:T(8,128)(2,1)S(1)} %slice.9), channel_id=1, source_target_pairs={{0,6},{2,0},{4,2},{6,4},{1,7},{3,1},{5,3},{7,5},{8,14},{10,8},{12,... | collective-permute-start | bytes 1572872 | tf_op jit(solution)/shard_map/ppermute | solution.py:376
  42.8 0.0 collective-permute-start.11
  42.8 0.5 collective-permute-start.12
  43.3 1.3 %collective-permute-start.13 = (bf16[1056,128]{1,0:T(8,128)(2,1)}, bf16[1056,128]{1,0:T(8,128)(2,1)S(1)}, u32[]{:S(2)}, u32[]{:S(2)}) collective-permute-start(bf16[1056,128]{1,0:T(8,128)(2,1)} %get-tuple-element.58), channel_id=1, source_target_pairs={{0,192},{64,128},{128,64},{192,0},{1,193},{65,129},{129,65},{193,1... | collective-permute-start | bytes 811016 | tf_op jit(solution)/shard_map/ppermute | solution.py:379
  44.6 1.8 %attend_near.2 = (f32[8,128]{1,0:T(8,128)S(1)}, f32[8,128]{1,0:T(8,128)S(1)}, f32[8,128,128]{2,1,0:T(8,128)S(1)}) custom-call(s32[1]{0:T(128)} %bitcast.1.y_ref, bf16[8,3,128,128]{3,2,1,0:T(8,128)(2,1)S(1)} %all-to-all-done.own_ref.refs_0_, bf16[8,3,128,128]{3,2,1,0:T(8,128)(2,1)S(1)} %all-to-all-done.own_ref.refs_0_), custom_call_target="tpu_custom_call" | custom-call | flops 350000000 | bytes 1500000 | tf_op jit(solution)/shard_map/attend_near/pallas_call | solution.py:131
  46.4 6.4 %collective-permute-done.7.refs_0_ = bf16[8,2,128,128]{3,2,1,0:T(8,128)(2,1)S(1)} collective-permute-done((bf16[8,2,128,128]{3,2,1,0:T(8,128)(2,1)S(1)}, bf16[8,2,128,128]{3,2,1,0:T(8,128)(2,1)S(1)}, u32[]{:S(2)}, u32[]{:S(2)}) %collective-permute-start.7) | collective-permute-done | bytes 524320 | tf_op jit(solution)/shard_map/ppermute | solution.py:375
  52.9 3.0 %collective-permute-start.10 = (bf16[4,2,128,128]{3,2,1,0:T(8,128)(2,1)S(1)}, bf16[4,2,128,128]{3,2,1,0:T(8,128)(2,1)S(1)}, u32[]{:S(2)}, u32[]{:S(2)}) collective-permute-start(bf16[4,2,128,128]{3,2,1,0:T(8,128)(2,1)S(1)} %slice.11), channel_id=1, source_target_pairs={{0,6},{2,0},{4,2},{6,4},{1,7},{3,1},{5,3},{7,5},{8,14},{10,8},{12,... | collective-permute-start | bytes 786440 | tf_op jit(solution)/shard_map/ppermute | solution.py:384
  55.9 0.3 collective-permute-start.9
  56.2 3.3 %attend_near.3 = (f32[8,128]{1,0:T(8,128)S(1)}, f32[8,128]{1,0:T(8,128)S(1)}, f32[8,128,128]{2,1,0:T(8,128)S(1)}) custom-call(s32[1]{0:T(128)} %bitcast.1.y_ref, bf16[8,3,128,128]{3,2,1,0:T(8,128)(2,1)S(1)} %all-to-all-done.own_ref.refs_0_, bf16[8,2,128,128]{3,2,1,0:T(8,128)(2,1)S(1)} %collective-permute-done.7.refs_0_, ...), custom_call_target="tpu_custom_call" | custom-call | flops 700000000 | bytes 1500000 | tf_op jit(solution)/shard_map/attend_near/pallas_call | solution.py:131
  59.5 0.0 collective-permute-done.12.refs_2_
  59.5 0.0 collective-permute-done.13.refs_3_
  59.6 0.3 collective-permute-done.10.refs_1_
  59.8 4.0 %collective-permute-done.9.refs_0_ = bf16[4,2,128,128]{3,2,1,0:T(8,128)(2,1)S(1)} collective-permute-done((bf16[4,2,128,128]{3,2,1,0:T(8,128)(2,1)S(1)}, bf16[4,2,128,128]{3,2,1,0:T(8,128)(2,1)S(1)}, u32[]{:S(2)}, u32[]{:S(2)}) %collective-permute-start.9) | collective-permute-done | bytes 262176 | tf_op jit(solution)/shard_map/ppermute | solution.py:383
  63.8 2.5 %attend_far.1 = bf16[8,128,128]{2,1,0:T(8,128)(2,1)} custom-call(s32[1]{0:T(128)} %bitcast.1.y_ref, bf16[8,3,128,128]{3,2,1,0:T(8,128)(2,1)S(1)} %all-to-all-done.own_ref.refs_0_, bf16[4,2,128,128]{3,2,1,0:T(8,128)(2,1)S(1)} %collective-permute-done.9.refs_0_, bf16[4,2,128,128]{3,2,1,0:T(8,128)(2,1)S(1)} %collective-permute-done.10.refs_1_, ...), custom_call_target="tpu_custom_call" | custom-call | flops 350000000 | bytes 1500000 | tf_op jit(solution)/shard_map/attend_far/pallas_call | solution.py:131
  66.3 5.4 %all-to-all-start.1 = ((bf16[8,128,128]{2,1,0:T(8,128)(2,1)}), bf16[8,128,128]{2,1,0:T(8,128)(2,1)S(1)}, u32[]{:S(2)}, u32[]{:S(2)}) async-start(bf16[8,128,128]{2,1,0:T(8,128)(2,1)} %attend_far.1), calls=%async_computation.1 | async-start | bytes 524288 | tf_op jit(solution)/shard_map/all_to_all | solution.py:391
  71.7 12.6 %all-to-all-done.1.self_ref = bf16[8,128,128]{2,1,0:T(8,128)(2,1)S(1)} async-done(((bf16[8,128,128]{2,1,0:T(8,128)(2,1)}), bf16[8,128,128]{2,1,0:T(8,128)(2,1)S(1)}, u32[]{:S(2)}, u32[]{:S(2)}) %all-to-all-start.1) | async-done | bytes 262176 | tf_op jit(solution)/shard_map/all_to_all | solution.py:391
  84.4 0.3 join.1
  84.7 2.9 %fusion.7 = bf16[128,2048]{1,0:T(8,128)(2,1)S(1)} fusion(bf16[128,1024]{1,0:T(8,128)(2,1)S(1)} %join.1, bf16[1024,4096]{1,0:T(8,128)(2,1)} %param.13, s32[]{:T(128)S(6)} %select_n.7), kind=kOutput, calls=%fused_computation.5 | convolution fusion | flops 537133056 | bytes 4980740 | tf_op jit(solution)/shard_map/dot_general | solution.py:398
  87.6 2.2 %collective-permute-start.14 = (bf16[128,2048]{1,0:T(8,128)(2,1)S(1)}, bf16[128,2048]{1,0:T(8,128)(2,1)S(1)}, u32[]{:S(2)}, u32[]{:S(2)}) collective-permute-start(bf16[128,2048]{1,0:T(8,128)(2,1)S(1)} %fusion.7), channel_id=1, source_target_pairs={{0,1},{1,0},{2,3},{3,2},{4,5},{5,4},{6,7},{7,6},{8,9},{9,8},{10,11... | collective-permute-start | bytes 1572872 | tf_op jit(solution)/shard_map/ppermute | solution.py:400
  89.8 2.9 %fusion.4.kept_ref = bf16[128,2048]{1,0:T(8,128)(2,1)S(1)} fusion(bf16[128,1024]{1,0:T(8,128)(2,1)S(1)} %join.1, bf16[1024,4096]{1,0:T(8,128)(2,1)} %param.13, s32[]{:T(128)S(6)} %select_n.6), kind=kOutput, calls=%fused_computation.4 | convolution fusion | flops 537133056 | bytes 4980740 | tf_op jit(solution)/shard_map/dot_general | solution.py:398
  92.8 10.4 %collective-permute-done.14.received_ref = bf16[128,2048]{1,0:T(8,128)(2,1)S(1)} collective-permute-done((bf16[128,2048]{1,0:T(8,128)(2,1)S(1)}, bf16[128,2048]{1,0:T(8,128)(2,1)S(1)}, u32[]{:S(2)}, u32[]{:S(2)}) %collective-permute-start.14) | collective-permute-done | bytes 524320 | tf_op jit(solution)/shard_map/ppermute | solution.py:400
  103.1 0.8 add.17
  (17 shorter events, 0.1 us)
Async XLA Ops:
  0.0 5.7 %collective-permute-start = (s32[1,2,2,2]{3,2,1,0:T(2,128)}, s32[1,2,2,2]{3,2,1,0:T(2,128)S(1)}, u32[]{:S(2)}, u32[]{:S(2)}) collective-permute-start(s32[1,2,2,2]{3,2,1,0:T(2,128)} %param.11), channel_id=1, source_target_pairs={{0,2},{2,4},{4,6},{6,8},{8,10},{10,12},{12,14},{14,16},{16,18},{18... | collective-permute-start | bytes 104 | tf_op jit(solution)/shard_map/ppermute | solution.py:350
  5.7 33.7 %all-to-all-start = ((bf16[8,3,128,128]{3,2,1,0:T(8,128)(2,1)}), bf16[8,3,128,128]{3,2,1,0:T(8,128)(2,1)S(1)}, u32[]{:S(2)}, u32[]{:S(2)}) async-start(bf16[8,3,128,128]{3,2,1,0:T(8,128)(2,1)} %split_heads.1), calls=%async_computation | async-start | bytes 1572864 | tf_op jit(solution)/shard_map/all_to_all | solution.py:353
  17.5 3.0 %collective-permute-start.4 = (bf16[128,1024]{1,0:T(8,128)(2,1)}, bf16[128,1024]{1,0:T(8,128)(2,1)S(1)}, u32[]{:S(2)}, u32[]{:S(2)}) collective-permute-start(bf16[128,1024]{1,0:T(8,128)(2,1)} %bitcast.16), channel_id=1, source_target_pairs={{0,64},{64,0},{1,65},{65,1},{2,66},{66,2},{3,67},{67,3},{4,68},{68... | collective-permute-start | bytes 786440 | tf_op jit(solution)/shard_map/ppermute | solution.py:358
  17.5 9.0 %collective-permute-start.1 = (bf16[128,1024]{1,0:T(8,128)(2,1)}, bf16[128,1024]{1,0:T(8,128)(2,1)S(1)}, u32[]{:S(2)}, u32[]{:S(2)}) collective-permute-start(bf16[128,1024]{1,0:T(8,128)(2,1)} %bitcast.17), channel_id=1, source_target_pairs={{0,128},{128,0},{1,129},{129,1},{2,130},{130,2},{3,131},{131,3},{4... | collective-permute-start | bytes 786440 | tf_op jit(solution)/shard_map/ppermute | solution.py:357
  18.8 1.7 %copy-start.1 = (s32[2,2,2,2]{3,2,1,0:T(2,128)}, s32[2,2,2,2]{3,2,1,0:T(2,128)S(1)}, u32[]{:S(2)}) copy-start(s32[2,2,2,2]{3,2,1,0:T(2,128)S(1)} %constant_dynamic-update-slice_fusion.ids0_ref) | copy-start | bytes 196
  18.8 1.7 %collective-permute-start.3 = (s32[2,2,2,2]{3,2,1,0:T(2,128)S(1)}, s32[2,2,2,2]{3,2,1,0:T(2,128)S(1)}, u32[]{:S(2)}, u32[]{:S(2)}) collective-permute-start(s32[2,2,2,2]{3,2,1,0:T(2,128)S(1)} %constant_dynamic-update-slice_fusion.ids0_ref), channel_id=1, source_target_pairs={{0,64},{64,0},{1,65},{65,1},{2,66},{66,2},{3,67},{67,3},{4,68},{68... | collective-permute-start | bytes 200 | tf_op jit(solution)/shard_map/ppermute | solution.py:360
  18.9 7.6 %collective-permute-start.2 = (s32[2,2,2,2]{3,2,1,0:T(2,128)S(1)}, s32[2,2,2,2]{3,2,1,0:T(2,128)S(1)}, u32[]{:S(2)}, u32[]{:S(2)}) collective-permute-start(s32[2,2,2,2]{3,2,1,0:T(2,128)S(1)} %constant_dynamic-update-slice_fusion.ids0_ref), channel_id=1, source_target_pairs={{0,128},{128,0},{1,129},{129,1},{2,130},{130,2},{3,131},{131,3},{4... | collective-permute-start | bytes 200 | tf_op jit(solution)/shard_map/ppermute | solution.py:359
  20.5 0.6 copy-start.6
  20.5 0.7 copy-start.3
  25.6 58.8 %copy-start = (bf16[1056,128]{1,0:T(8,128)(2,1)S(1)}, bf16[1056,128]{1,0:T(8,128)(2,1)}, u32[]{:S(2)}) copy-start(bf16[1056,128]{1,0:T(8,128)(2,1)} %get-tuple-element.38.refs_0_) | copy-start | bytes 811012
  26.5 1.6 %copy-start.5 = (s32[2,2,2,2]{3,2,1,0:T(2,128)}, s32[2,2,2,2]{3,2,1,0:T(2,128)S(1)}, u32[]{:S(2)}) copy-start(s32[2,2,2,2]{3,2,1,0:T(2,128)S(1)} %collective-permute-done.2.ids0_ref) | copy-start | bytes 196
  26.5 1.6 %copy-start.2 = (bf16[128,1024]{1,0:T(8,128)(2,1)}, bf16[128,1024]{1,0:T(8,128)(2,1)S(1)}, u32[]{:S(2)}) copy-start(bf16[128,1024]{1,0:T(8,128)(2,1)S(1)} %collective-permute-done.1.q0_ref) | copy-start | bytes 786436
  26.5 1.6 %collective-permute-start.6 = (bf16[128,1024]{1,0:T(8,128)(2,1)S(1)}, bf16[128,1024]{1,0:T(8,128)(2,1)S(1)}, u32[]{:S(2)}, u32[]{:S(2)}) collective-permute-start(bf16[128,1024]{1,0:T(8,128)(2,1)S(1)} %collective-permute-done.1.q0_ref), channel_id=1, source_target_pairs={{0,64},{64,0},{1,65},{65,1},{2,66},{66,2},{3,67},{67,3},{4,68},{68... | collective-permute-start | bytes 786440 | tf_op jit(solution)/shard_map/ppermute | solution.py:365
  26.6 1.5 %collective-permute-start.5 = (s32[2,2,2,2]{3,2,1,0:T(2,128)S(1)}, s32[2,2,2,2]{3,2,1,0:T(2,128)S(1)}, u32[]{:S(2)}, u32[]{:S(2)}) collective-permute-start(s32[2,2,2,2]{3,2,1,0:T(2,128)S(1)} %collective-permute-done.2.ids0_ref), channel_id=1, source_target_pairs={{0,64},{64,0},{1,65},{65,1},{2,66},{66,2},{3,67},{67,3},{4,68},{68... | collective-permute-start | bytes 200 | tf_op jit(solution)/shard_map/ppermute | solution.py:366
  28.1 0.6 copy-start.7
  28.7 0.7 copy-start.4
  39.5 13.4 %collective-permute-start.7 = (bf16[8,2,128,128]{3,2,1,0:T(8,128)(2,1)S(1)}, bf16[8,2,128,128]{3,2,1,0:T(8,128)(2,1)S(1)}, u32[]{:S(2)}, u32[]{:S(2)}) collective-permute-start(bf16[8,2,128,128]{3,2,1,0:T(8,128)(2,1)S(1)} %slice.9), channel_id=1, source_target_pairs={{0,2},{2,4},{4,6},{6,0},{1,3},{3,5},{5,7},{7,1},{8,10},{10,12},{12... | collective-permute-start | bytes 1572872 | tf_op jit(solution)/shard_map/ppermute | solution.py:375
  39.6 13.3 %collective-permute-start.8 = (bf16[8,2,128,128]{3,2,1,0:T(8,128)(2,1)S(1)}, bf16[8,2,128,128]{3,2,1,0:T(8,128)(2,1)S(1)}, u32[]{:S(2)}, u32[]{:S(2)}) collective-permute-start(bf16[8,2,128,128]{3,2,1,0:T(8,128)(2,1)S(1)} %slice.9), channel_id=1, source_target_pairs={{0,6},{2,0},{4,2},{6,4},{1,7},{3,1},{5,3},{7,5},{8,14},{10,8},{12,... | collective-permute-start | bytes 1572872 | tf_op jit(solution)/shard_map/ppermute | solution.py:376
  42.8 16.7 %collective-permute-start.11 = (bf16[1056,128]{1,0:T(8,128)(2,1)}, bf16[1056,128]{1,0:T(8,128)(2,1)S(1)}, u32[]{:S(2)}, u32[]{:S(2)}) collective-permute-start(bf16[1056,128]{1,0:T(8,128)(2,1)} %get-tuple-element.56), channel_id=1, source_target_pairs={{0,64},{64,0},{1,65},{65,1},{2,66},{66,2},{3,67},{67,3},{4,68},{68... | collective-permute-start | bytes 811016 | tf_op jit(solution)/shard_map/ppermute | solution.py:377
  42.8 16.8 %collective-permute-start.12 = (bf16[1056,128]{1,0:T(8,128)(2,1)}, bf16[1056,128]{1,0:T(8,128)(2,1)S(1)}, u32[]{:S(2)}, u32[]{:S(2)}) collective-permute-start(bf16[1056,128]{1,0:T(8,128)(2,1)} %get-tuple-element.57), channel_id=1, source_target_pairs={{0,128},{128,0},{1,129},{129,1},{2,130},{130,2},{3,131},{131,3},{4... | collective-permute-start | bytes 811016 | tf_op jit(solution)/shard_map/ppermute | solution.py:378
  43.3 16.2 %collective-permute-start.13 = (bf16[1056,128]{1,0:T(8,128)(2,1)}, bf16[1056,128]{1,0:T(8,128)(2,1)S(1)}, u32[]{:S(2)}, u32[]{:S(2)}) collective-permute-start(bf16[1056,128]{1,0:T(8,128)(2,1)} %get-tuple-element.58), channel_id=1, source_target_pairs={{0,192},{64,128},{128,64},{192,0},{1,193},{65,129},{129,65},{193,1... | collective-permute-start | bytes 811016 | tf_op jit(solution)/shard_map/ppermute | solution.py:379
  52.9 6.9 %collective-permute-start.10 = (bf16[4,2,128,128]{3,2,1,0:T(8,128)(2,1)S(1)}, bf16[4,2,128,128]{3,2,1,0:T(8,128)(2,1)S(1)}, u32[]{:S(2)}, u32[]{:S(2)}) collective-permute-start(bf16[4,2,128,128]{3,2,1,0:T(8,128)(2,1)S(1)} %slice.11), channel_id=1, source_target_pairs={{0,6},{2,0},{4,2},{6,4},{1,7},{3,1},{5,3},{7,5},{8,14},{10,8},{12,... | collective-permute-start | bytes 786440 | tf_op jit(solution)/shard_map/ppermute | solution.py:384
  55.9 7.8 %collective-permute-start.9 = (bf16[4,2,128,128]{3,2,1,0:T(8,128)(2,1)S(1)}, bf16[4,2,128,128]{3,2,1,0:T(8,128)(2,1)S(1)}, u32[]{:S(2)}, u32[]{:S(2)}) collective-permute-start(bf16[4,2,128,128]{3,2,1,0:T(8,128)(2,1)S(1)} %slice.10), channel_id=1, source_target_pairs={{0,2},{2,4},{4,6},{6,0},{1,3},{3,5},{5,7},{7,1},{8,10},{10,12},{12... | collective-permute-start | bytes 786440 | tf_op jit(solution)/shard_map/ppermute | solution.py:383
  66.3 18.1 %all-to-all-start.1 = ((bf16[8,128,128]{2,1,0:T(8,128)(2,1)}), bf16[8,128,128]{2,1,0:T(8,128)(2,1)S(1)}, u32[]{:S(2)}, u32[]{:S(2)}) async-start(bf16[8,128,128]{2,1,0:T(8,128)(2,1)} %attend_far.1), calls=%async_computation.1 | async-start | bytes 524288 | tf_op jit(solution)/shard_map/all_to_all | solution.py:391
  87.6 15.5 %collective-permute-start.14 = (bf16[128,2048]{1,0:T(8,128)(2,1)S(1)}, bf16[128,2048]{1,0:T(8,128)(2,1)S(1)}, u32[]{:S(2)}, u32[]{:S(2)}) collective-permute-start(bf16[128,2048]{1,0:T(8,128)(2,1)S(1)} %fusion.7), channel_id=1, source_target_pairs={{0,1},{1,0},{2,3},{3,2},{4,5},{5,4},{6,7},{7,6},{8,9},{9,8},{10,11... | collective-permute-start | bytes 1572872 | tf_op jit(solution)/shard_map/ppermute | solution.py:400
where the time goes:
time: 103 us; the launch traced here: 104 us
  waiting for transfers between devices  42.4 us (41%)
  starting transfers between devices  34.2 us (33%)
  Pallas kernels  18.6 us (18%)
  matrix products  5.82 us (6%)
  local copies, waits for them, and re-layouts  2.74 us (3%)
    all_to_all x1, waiting for transfers between devices, per_device(): self_t = lax.all_to_all(self_t, 'z', 0, 0, tiled=True)  12.6 us
    all_to_all x1, starting transfers between devices, per_device(): own = lax.all_to_all(own, 'z', 0, 0, tiled=True)  11.8 us
    ppermute x1, waiting for transfers between devices, per_device(): received = lax.ppermute(projected(1 - xh), 'xh', ring('xh', 1))  10.4 us
    pallas_call x2, Pallas kernels, cross_attend(): pl.pallas_call(cross_kernel, out_shape=(shape,) * 2, in_specs=[SMEM] * 3...  7.6 us
    pallas_call x3, Pallas kernels, attend(): pl.pallas_call(functools.partial(attend_kernel, steps, len(parts), not st...  7.59 us
    all_to_all x1, waiting for transfers between devices, per_device(): own = lax.all_to_all(own, 'z', 0, 0, tiled=True)  6.81 us
    ppermute x1, waiting for transfers between devices, per_device(): below = lax.ppermute(kv, 'y', up)  6.42 us
    dot_general x2, matrix products, projected(): return jnp.dot(attended, columns, preferred_element_type=F32).astype(BF16)  5.82 us
  transfers between devices with their start and end apart: 17, of which 8 were waited for; matrix products, arithmetic and copies ran while one was open for 3% of the time, Pallas kernels for 14%

commit v1 on v0

--- a/solution.py
+++ b/solution.py
@@ -235,11 +235,7 @@
         for h in range(HEADS):
             out_ref[h * HD : (h + 1) * HD, :] = (summed[h] * inverse[h : h + 1, :]).astype(BF16)
         level = jnp.where(some, top[...] * EXP2_SCALE + jnp.log2(safe), LOW)
-        high = level.astype(BF16).astype(F32)
-        middle = (level - high).astype(BF16).astype(F32)
-        low = level - high - middle
-        stats = jnp.concatenate([high, middle, low, jnp.zeros_like(low)], axis=0)
-        out_ref[HEADS * HD :, :] = stats.astype(BF16)
+        store_level(out_ref, level)
 
 
 def cross_attend(place, ids, queries, database):
@@ -266,17 +262,53 @@
     )(*ids, place, *queries, database)
 
 
+def level_of(part_ref):
+    stats = part_ref[HEADS * HD :, :].astype(F32)
+    return stats[0:8] + stats[8:16] + stats[16:24]
+
+
+def store_level(out_ref, level):
+    high = level.astype(BF16).astype(F32)
+    middle = (level - high).astype(BF16).astype(F32)
+    low = level - high - middle
+    stats = jnp.concatenate([high, middle, low, jnp.zeros_like(low)], axis=0)
+    out_ref[HEADS * HD :, :] = stats.astype(BF16)
+
+
+def merge_kernel(first_ref, second_ref, out_ref):
+    levels = [level_of(first_ref), level_of(second_ref)]
+    top = jnp.maximum(*levels)
+    shares = [jnp.exp2(level - top) for level in levels]
+    whole = shares[0] + shares[1]
+    shares = [share / whole for share in shares]
+    for h in range(HEADS):
+        cols = slice(h * HD, (h + 1) * HD)
+        first = first_ref[cols, :].astype(F32) * shares[0][h : h + 1, :]
+        second = second_ref[cols, :].astype(F32) * shares[1][h : h + 1, :]
+        out_ref[cols, :] = (first + second).astype(BF16)
+    store_level(out_ref, top + jnp.log2(whole))
+
+
+def merge(first, second):
+    return pl.pallas_call(
+        merge_kernel,
+        out_shape=jax.ShapeDtypeStruct(first.shape, BF16),
+        in_specs=[VMEM] * 2,
+        out_specs=VMEM,
+        compiler_params=params(),
+        name="merge",
+        cost_estimate=pl.CostEstimate(flops=0, bytes_accessed=800_000, transcendentals=4096),
+    )(first, second)
+
+
 COLS = 2048
 
 
 def join_kernel(place_ref, self_ref, *refs):
-    part_refs, att_ref = refs[0:4], refs[4]
+    part_refs, att_ref = refs[0:3], refs[3]
     row = lax.broadcasted_iota(jnp.int32, (1, ROWS), 1)
     live = jnp.where((row >= 63) | (place_ref[0] > 0), 1.0, 0.0).astype(F32)
-    levels = []
-    for part in part_refs:
-        stats = part[HEADS * HD :, :].astype(F32)
-        levels.append(stats[0:8] + stats[8:16] + stats[16:24])
+    levels = [level_of(part) for part in part_refs]
     top = functools.reduce(jnp.maximum, levels)
     shares = [jnp.exp2(level - top) for level in levels]
     whole = functools.reduce(jnp.add, shares)
@@ -293,7 +325,7 @@
     return pl.pallas_call(
         join_kernel,
         out_shape=jax.ShapeDtypeStruct((ROWS, HEADS * HD), BF16),
-        in_specs=[SMEM] + [VMEM] * 5,
+        in_specs=[SMEM] + [VMEM] * 4,
         out_specs=VMEM,
         compiler_params=params(),
         name="join",
@@ -304,14 +336,17 @@
 PIECES = 4
 
 
-def add_kernel(kept_ref, received_ref, out_ref, buffer, done):
+def add_kernel(kept0_ref, kept1_ref, received0_ref, received1_ref, out_ref, buffer, done):
     wide = COLS // PIECES
     copies = []
     for piece in range(PIECES):
         cols = slice(piece * wide, (piece + 1) * wide)
-        buffer[:, cols] = (kept_ref[:, cols].astype(F32) + received_ref[:, cols].astype(F32)).astype(
-            BF16
+        kept_ref, received_ref = (
+            (kept0_ref, received0_ref) if 2 * piece < PIECES else (kept1_ref, received1_ref)
         )
+        inner = slice(cols.start % (COLS // 2), cols.start % (COLS // 2) + wide)
+        kept, received = kept_ref[:, inner].astype(F32), received_ref[:, inner].astype(F32)
+        buffer[:, cols] = (kept + received).astype(BF16)
         copies.append(
             pltpu.make_async_copy(buffer.at[:, cols], out_ref.at[:, cols], done.at[piece])
         )
@@ -324,13 +359,13 @@
     return pl.pallas_call(
         add_kernel,
         out_shape=jax.ShapeDtypeStruct((ROWS, COLS), BF16),
-        in_specs=[VMEM] * 2,
+        in_specs=[VMEM] * 4,
         out_specs=pl.BlockSpec(memory_space=pl.ANY),
         scratch_shapes=[pltpu.VMEM((ROWS, COLS), BF16), pltpu.SemaphoreType.DMA((PIECES,))],
         compiler_params=params(),
         name="add",
         cost_estimate=pl.CostEstimate(flops=0, bytes_accessed=1_500_000, transcendentals=0),
-    )(kept, received)
+    )(*kept, *received)
 
 
 def ring(axis, step):
@@ -367,38 +402,45 @@
     across_part, diagonal_part = cross_attend(
         place_dp, (ids_across, ids_diagonal), (from_across, from_diagonal), database[0]
     )
-    own, across_part, diagonal_part, beside_part = lax.optimization_barrier(
-        (own, across_part, diagonal_part, beside_part)
-    )
-
-    kv = own[:, :2]
-    below = lax.ppermute(kv, "y", up)
-    above = lax.ppermute(kv, "y", down)
     beside_part = lax.ppermute(beside_part, "core", beside)
+    diagonal_part = lax.ppermute(diagonal_part, "core", beside)
+    own, _, _ = lax.optimization_barrier((own, across_part, beside_part))
+
+    half = ZS // 2
+    kv_low, kv_high = own[:half, :2], own[half:, :2]
+    below_low = lax.ppermute(kv_low, "y", up)
+    above_high = lax.ppermute(kv_high, "y", down)
+    below_high = lax.ppermute(kv_high, "y", up)
+    above_low = lax.ppermute(kv_low, "y", down)
+    across_part = merge(across_part, diagonal_part)
+    below_low, above_high, own, across_part = lax.optimization_barrier(
+        (below_low, above_high, own, across_part)
+    )
+
+    far_low = lax.ppermute(below_low, "y", up)
+    far_high = lax.ppermute(above_high, "y", down)
     across_part = lax.ppermute(across_part, "xl", across)
-    diagonal_part = lax.ppermute(diagonal_part, dp, [(i, 3 - i) for i in range(4)])
     state = attend(y_index, own, (0,), (own,))
-    below, above, state = lax.optimization_barrier((below, above, state))
-
-    far_low = lax.ppermute(below[: ZS // 2], "y", up)
-    far_high = lax.ppermute(above[ZS // 2 :], "y", down)
-    state = attend(y_index, own, (YS - 1, 1), (below, above), state)
-    far_low, far_high, state, beside_part, across_part, diagonal_part = lax.optimization_barrier(
-        (far_low, far_high, state, beside_part, across_part, diagonal_part)
+    near = (below_low, below_high, above_low, above_high)
+    state = attend(y_index, own, (YS - 1, 1), near, state)
+    far_low, far_high, state, across_part = lax.optimization_barrier(
+        (far_low, far_high, state, across_part)
     )
 
     self_t = attend(y_index, own, (2,), (far_low, far_high), state, last=True)
     self_t = lax.all_to_all(self_t, "z", 0, 0, tiled=True)
 
-    attended = join(seq_index, self_t, (own_part, beside_part, across_part, diagonal_part))
+    attended = join(seq_index, self_t, (own_part, beside_part, across_part))
     xh = lax.axis_index("xh")
 
     def projected(half):
-        columns = lax.dynamic_slice_in_dim(out_weight, half * COLS, COLS, axis=1)
+        columns = lax.dynamic_slice_in_dim(out_weight, half * (COLS // 2), COLS // 2, axis=1)
         return jnp.dot(attended, columns, preferred_element_type=F32).astype(BF16)
 
-    received = lax.ppermute(projected(1 - xh), "xh", ring("xh", 1))
-    return add(projected(xh), received)[None]
+    received = [
+        lax.ppermute(projected(2 * (1 - xh) + piece), "xh", ring("xh", 1)) for piece in range(2)
+    ]
+    return add([projected(2 * xh + piece) for piece in range(2)], received)[None]
 
 
 def solution(mesh):

time: 103 us -> 97.7 us (0.949); the launches traced: 104 us -> 96.5 us
  waiting for transfers between devices: 42.4 us -> 26.1 us
  starting transfers between devices: 34.2 us -> 37.7 us
  matrix products: 5.82 us -> 8.16 us
  local copies, waits for them, and re-layouts: 2.74 us -> 4.44 us
  Pallas kernels: 18.6 us -> 19.8 us
    ppermute x6 -> x9, waiting for transfers between devices: 21 us -> 6.86 us  [the longest x2 3.74 us: per_device(): lax.ppermute(projected(2 * (1 - xh) + piece), 'xh', ring('xh', 1))]
    ppermute x6 -> x9, starting transfers between devices: 10.1 us -> 13.5 us  [the longest x2 3.7 us: per_device(): lax.ppermute(projected(2 * (1 - xh) + piece), 'xh', ring('xh', 1))]
    dot_general x2 -> x4, matrix products: 5.82 us -> 8.16 us  [projected(): return jnp.dot(attended, columns, preferred_element_type=F32).astype(BF16)]
    all_to_all x1, waiting for transfers between devices: 6.81 us -> 4.56 us  [per_device(): own = lax.all_to_all(own, 'z', 0, 0, tiled=True)]
    pallas_call x2, Pallas kernels: 7.6 us -> 8.69 us  [cross_attend(): pl.pallas_call(cross_kernel, out_shape=(shape,) * 2, in_specs=[SMEM] * 3...]
    unnamed x17 -> x19, local copies, waits for them, and re-layouts: 1.98 us -> 2.93 us
  transfers between devices with their start and end apart: 17 -> 20, of which waited for: 8 -> 6; matrix products, arithmetic and copies ran while one was open for 3% -> 8% of each run, Pallas kernels for 14% -> 17%
where the time goes in v1:
time: 97.7 us; the launch traced here: 96.5 us
  starting transfers between devices  37.7 us (39%)
  waiting for transfers between devices  26.1 us (27%)
  Pallas kernels  19.8 us (20%)
  matrix products  8.16 us (8%)
  local copies, waits for them, and re-layouts  4.44 us (5%)
    all_to_all x1, starting transfers between devices, per_device(): own = lax.all_to_all(own, 'z', 0, 0, tiled=True)  11.8 us
    all_to_all x1, waiting for transfers between devices, per_device(): self_t = lax.all_to_all(self_t, 'z', 0, 0, tiled=True)  11.7 us
    pallas_call x2, Pallas kernels, cross_attend(): pl.pallas_call(cross_kernel, out_shape=(shape,) * 2, in_specs=[SMEM] * 3...  8.69 us
    dot_general x4, matrix products, projected(): return jnp.dot(attended, columns, preferred_element_type=F32).astype(BF16)  8.16 us
    pallas_call x3, Pallas kernels, attend(): pl.pallas_call(functools.partial(attend_kernel, steps, len(parts), not st...  7.6 us
    all_to_all x1, starting transfers between devices, per_device(): self_t = lax.all_to_all(self_t, 'z', 0, 0, tiled=True)  5.13 us
    all_to_all x1, waiting for transfers between devices, per_device(): own = lax.all_to_all(own, 'z', 0, 0, tiled=True)  4.56 us
    ppermute x2, waiting for transfers between devices, per_device(): lax.ppermute(projected(2 * (1 - xh) + piece), 'xh', ring('xh', 1))  3.74 us
  transfers between devices with their start and end apart: 20, of which 6 were waited for; matrix products, arithmetic and copies ran while one was open for 8% of the time, Pallas kernels for 17%

profile of v1, /device:TPU:2, one launch (start us, length us, event | category | flops | bytes accessed | tf_op | source)
XLA Modules:
  0.0 96.5 jit_solution(7377410115075500480)
XLA Ops:
  0.0 3.5 %collective-permute-start = (s32[1,2,2,2]{3,2,1,0:T(2,128)}, s32[1,2,2,2]{3,2,1,0:T(2,128)S(1)}, u32[]{:S(2)}, u32[]{:S(2)}) collective-permute-start(s32[1,2,2,2]{3,2,1,0:T(2,128)} %param.11), channel_id=1, source_target_pairs={{0,2},{2,4},{4,6},{6,8},{8,10},{10,12},{12,14},{14,16},{16,18},{18... | collective-permute-start | bytes 104 | tf_op jit(solution)/shard_map/ppermute | solution.py:385
  3.5 2.2 %split_heads.1 = bf16[8,3,128,128]{3,2,1,0:T(8,128)(2,1)} custom-call(bf16[128,1024]{1,0:T(8,128)(2,1)} %bitcast.13, bf16[128,1024]{1,0:T(8,128)(2,1)} %bitcast.14, bf16[128,1024]{1,0:T(8,128)(2,1)} %bitcast.15), custom_call_target="tpu_custom_call" | custom-call | bytes 1572864 | tf_op jit(solution)/shard_map/split_heads/pallas_call | solution.py:44
  5.7 0.0 collective-permute-done
  5.7 11.8 %all-to-all-start = ((bf16[8,3,128,128]{3,2,1,0:T(8,128)(2,1)}), bf16[8,3,128,128]{3,2,1,0:T(8,128)(2,1)S(1)}, u32[]{:S(2)}, u32[]{:S(2)}) async-start(bf16[8,3,128,128]{3,2,1,0:T(8,128)(2,1)} %split_heads.1), calls=%async_computation | async-start | bytes 1572864 | tf_op jit(solution)/shard_map/all_to_all | solution.py:388
  17.5 0.0 collective-permute-start.4
  17.5 0.6 collective-permute-start.1
  18.1 0.7 constant_dynamic-update-slice_fusion.ids0_ref
  18.8 0.1 collective-permute-start.3
  18.9 1.5 %collective-permute-start.2 = (s32[2,2,2,2]{3,2,1,0:T(2,128)S(1)}, s32[2,2,2,2]{3,2,1,0:T(2,128)S(1)}, u32[]{:S(2)}, u32[]{:S(2)}) collective-permute-start(s32[2,2,2,2]{3,2,1,0:T(2,128)S(1)} %constant_dynamic-update-slice_fusion.ids0_ref), channel_id=1, source_target_pairs={{0,128},{128,0},{1,129},{129,1},{2,130},{130,2},{3,131},{131,3},{4... | collective-permute-start | bytes 200 | tf_op jit(solution)/shard_map/ppermute | solution.py:394
  20.4 0.0 collective-permute-done.3.ids1_ref
  20.5 0.0 collective-permute-done.4.q1_ref
  20.5 0.6 copy-done.7
  21.0 0.1 copy-done.4
  21.2 3.8 %cross_attend.2 = (bf16[1056,128]{1,0:T(8,128)(2,1)}, bf16[1056,128]{1,0:T(8,128)(2,1)}) custom-call(s32[2,2,2,2]{3,2,1,0:T(2,128)} %copy-done.2, s32[2,2,2,2]{3,2,1,0:T(2,128)} %copy-done.7, s32[1]{0:T(128)} %bitcast.6.place_ref, bf16[128,1024]{1,0:T(8,128)(2,1)} %bitcast.20, bf16[128,1024]{1,0:T(8,128)(2,1)} %copy-done.4, bf16[2,6,128,1024]{3,2,1,0:T(8,128)(2,1)} %bitcast.16), custom_call_target="tpu_custom_call" | custom-call | flops 2000000000 | bytes 5000000 | tf_op jit(solution)/shard_map/cross_attend/pallas_call | solution.py:243
  24.9 0.0 copy-start
  24.9 1.6 %collective-permute-done.2.ids0_ref = s32[2,2,2,2]{3,2,1,0:T(2,128)S(1)} collective-permute-done((s32[2,2,2,2]{3,2,1,0:T(2,128)S(1)}, s32[2,2,2,2]{3,2,1,0:T(2,128)S(1)}, u32[]{:S(2)}, u32[]{:S(2)}) %collective-permute-start.2) | collective-permute-done | bytes 96 | tf_op jit(solution)/shard_map/ppermute | solution.py:394
  26.5 0.1 collective-permute-start.6
  26.6 0.5 collective-permute-start.7
  27.1 0.1 collective-permute-start.5
  27.2 1.3 %collective-permute-done.5.ids1_ref = s32[2,2,2,2]{3,2,1,0:T(2,128)S(1)} collective-permute-done((s32[2,2,2,2]{3,2,1,0:T(2,128)S(1)}, s32[2,2,2,2]{3,2,1,0:T(2,128)S(1)}, u32[]{:S(2)}, u32[]{:S(2)}) %collective-permute-start.5) | collective-permute-done | bytes 96 | tf_op jit(solution)/shard_map/ppermute | solution.py:401
  28.5 0.6 copy-done.8
  29.1 0.7 copy-done.5
  29.8 4.9 %cross_attend.3 = (bf16[1056,128]{1,0:T(8,128)(2,1)}, bf16[1056,128]{1,0:T(8,128)(2,1)}) custom-call(s32[2,2,2,2]{3,2,1,0:T(2,128)} %copy-done.6, s32[2,2,2,2]{3,2,1,0:T(2,128)} %copy-done.8, s32[1]{0:T(128)} %bitcast.6.place_ref, bf16[128,1024]{1,0:T(8,128)(2,1)} %copy-done.3, bf16[128,1024]{1,0:T(8,128)(2,1)} %copy-done.5, bf16[2,6,128,1024]{3,2,1,0:T(8,128)(2,1)} %bitcast.17), custom_call_target="tpu_custom_call" | custom-call | flops 2000000000 | bytes 5000000 | tf_op jit(solution)/shard_map/cross_attend/pallas_call | solution.py:243
  34.8 0.1 collective-permute-start.10
  34.9 4.6 %all-to-all-done.own_ref.refs_0_ = bf16[8,3,128,128]{3,2,1,0:T(8,128)(2,1)S(1)} async-done(((bf16[8,3,128,128]{3,2,1,0:T(8,128)(2,1)}), bf16[8,3,128,128]{3,2,1,0:T(8,128)(2,1)S(1)}, u32[]{:S(2)}, u32[]{:S(2)}) %all-to-all-start) | async-done | bytes 786464 | tf_op jit(solution)/shard_map/all_to_all | solution.py:388
  39.4 0.8 fusion.24
  40.3 3.2 %collective-permute-start.9 = (bf16[4,2,128,128]{3,2,1,0:T(8,128)(2,1)}, bf16[4,2,128,128]{3,2,1,0:T(8,128)(2,1)S(1)}, u32[]{:S(2)}, u32[]{:S(2)}) collective-permute-start(bf16[4,2,128,128]{3,2,1,0:T(8,128)(2,1)} %get-tuple-element.55), channel_id=1, source_target_pairs={{0,6},{2,0},{4,2},{6,4},{1,7},{3,1},{5,3},{7,5},{8,14},{10,8},{12,... | collective-permute-start | bytes 786440 | tf_op jit(solution)/shard_map/ppermute | solution.py:412
  43.5 3.2 %collective-permute-start.14 = (bf16[4,2,128,128]{3,2,1,0:T(8,128)(2,1)}, bf16[4,2,128,128]{3,2,1,0:T(8,128)(2,1)S(1)}, u32[]{:S(2)}, u32[]{:S(2)}) collective-permute-start(bf16[4,2,128,128]{3,2,1,0:T(8,128)(2,1)} %get-tuple-element.56), channel_id=1, source_target_pairs={{0,6},{2,0},{4,2},{6,4},{1,7},{3,1},{5,3},{7,5},{8,14},{10,8},{12,... | collective-permute-start | bytes 786440 | tf_op jit(solution)/shard_map/ppermute | solution.py:414
  46.7 1.0 copy-done.1
  47.7 0.1 merge.1
  47.8 3.1 %collective-permute-done.8.refs_0_ = bf16[4,2,128,128]{3,2,1,0:T(8,128)(2,1)S(1)} collective-permute-done((bf16[4,2,128,128]{3,2,1,0:T(8,128)(2,1)}, bf16[4,2,128,128]{3,2,1,0:T(8,128)(2,1)S(1)}, u32[]{:S(2)}, u32[]{:S(2)}) %collective-permute-start.8) | collective-permute-done | bytes 262176 | tf_op jit(solution)/shard_map/ppermute | solution.py:411
  50.9 0.8 collective-permute-start.15
  51.7 3.3 %collective-permute-start.12 = (bf16[4,2,128,128]{3,2,1,0:T(8,128)(2,1)S(1)}, bf16[4,2,128,128]{3,2,1,0:T(8,128)(2,1)S(1)}, u32[]{:S(2)}, u32[]{:S(2)}) collective-permute-start(bf16[4,2,128,128]{3,2,1,0:T(8,128)(2,1)S(1)} %collective-permute-done.9.refs_3_), channel_id=1, source_target_pairs={{0,6},{2,0},{4,2},{6,4},{1,7},{3,1},{5,3},{7,5},{8,14},{10,8},{12,... | collective-permute-start | bytes 786440 | tf_op jit(solution)/shard_map/ppermute | solution.py:421
  55.0 1.8 %attend_near.2 = (f32[8,128]{1,0:T(8,128)S(1)}, f32[8,128]{1,0:T(8,128)S(1)}, f32[8,128,128]{2,1,0:T(8,128)S(1)}) custom-call(s32[1]{0:T(128)} %bitcast.1.y_ref, bf16[8,3,128,128]{3,2,1,0:T(8,128)(2,1)S(1)} %all-to-all-done.own_ref.refs_0_, bf16[8,3,128,128]{3,2,1,0:T(8,128)(2,1)S(1)} %all-to-all-done.own_ref.refs_0_), custom_call_target="tpu_custom_call" | custom-call | flops 350000000 | bytes 1500000 | tf_op jit(solution)/shard_map/attend_near/pallas_call | solution.py:131
  56.8 3.3 %attend_near.3 = (f32[8,128]{1,0:T(8,128)S(1)}, f32[8,128]{1,0:T(8,128)S(1)}, f32[8,128,128]{2,1,0:T(8,128)S(1)}) custom-call(s32[1]{0:T(128)} %bitcast.1.y_ref, bf16[8,3,128,128]{3,2,1,0:T(8,128)(2,1)S(1)} %all-to-all-done.own_ref.refs_0_, bf16[4,2,128,128]{3,2,1,0:T(8,128)(2,1)S(1)} %collective-permute-done.8.refs_0_, ...), custom_call_target="tpu_custom_call" | custom-call | flops 700000000 | bytes 1500000 | tf_op jit(solution)/shard_map/attend_near/pallas_call | solution.py:131
  60.2 2.5 %attend_far.1 = bf16[8,128,128]{2,1,0:T(8,128)(2,1)} custom-call(s32[1]{0:T(128)} %bitcast.1.y_ref, bf16[8,3,128,128]{3,2,1,0:T(8,128)(2,1)S(1)} %all-to-all-done.own_ref.refs_0_, bf16[4,2,128,128]{3,2,1,0:T(8,128)(2,1)S(1)} %collective-permute-done.11.refs_0_, bf16[4,2,128,128]{3,2,1,0:T(8,128)(2,1)S(1)} %collective-permute-done.12.refs_1_, ...), custom_call_target="tpu_custom_call" | custom-call | flops 350000000 | bytes 1500000 | tf_op jit(solution)/shard_map/attend_far/pallas_call | solution.py:131
  62.7 5.1 %all-to-all-start.1 = ((bf16[8,128,128]{2,1,0:T(8,128)(2,1)}), bf16[8,128,128]{2,1,0:T(8,128)(2,1)S(1)}, u32[]{:S(2)}, u32[]{:S(2)}) async-start(bf16[8,128,128]{2,1,0:T(8,128)(2,1)} %attend_far.1), calls=%async_computation.1 | async-start | bytes 524288 | tf_op jit(solution)/shard_map/all_to_all | solution.py:431
  67.8 11.7 %all-to-all-done.1.self_ref = bf16[8,128,128]{2,1,0:T(8,128)(2,1)S(1)} async-done(((bf16[8,128,128]{2,1,0:T(8,128)(2,1)}), bf16[8,128,128]{2,1,0:T(8,128)(2,1)S(1)}, u32[]{:S(2)}, u32[]{:S(2)}) %all-to-all-start.1) | async-done | bytes 262176 | tf_op jit(solution)/shard_map/all_to_all | solution.py:431
  79.6 0.3 join.1
  79.9 2.0 %fusion.17 = bf16[128,1024]{1,0:T(8,128)(2,1)S(1)} fusion(bf16[128,1024]{1,0:T(8,128)(2,1)S(1)} %join.1, bf16[1024,4096]{1,0:T(8,128)(2,1)} %param.13, s32[]{:T(128)S(6)} %select_n.15), kind=kOutput, calls=%fused_computation.11 | convolution fusion | flops 268566528 | bytes 2621444 | tf_op jit(solution)/shard_map/dot_general | solution.py:438
  81.9 2.2 %collective-permute-start.17 = (bf16[128,1024]{1,0:T(8,128)(2,1)S(1)}, bf16[128,1024]{1,0:T(8,128)(2,1)S(1)}, u32[]{:S(2)}, u32[]{:S(2)}) collective-permute-start(bf16[128,1024]{1,0:T(8,128)(2,1)S(1)} %fusion.17), channel_id=1, source_target_pairs={{0,1},{1,0},{2,3},{3,2},{4,5},{5,4},{6,7},{7,6},{8,9},{9,8},{10,11... | collective-permute-start | bytes 786440 | tf_op jit(solution)/shard_map/ppermute | solution.py:441
  84.1 2.0 %fusion.14 = bf16[128,1024]{1,0:T(8,128)(2,1)S(1)} fusion(bf16[128,1024]{1,0:T(8,128)(2,1)S(1)} %join.1, bf16[1024,4096]{1,0:T(8,128)(2,1)} %param.13, s32[]{:T(128)S(6)} %select_n.14), kind=kOutput, calls=%fused_computation.10 | convolution fusion | flops 268566528 | bytes 2621444 | tf_op jit(solution)/shard_map/dot_general | solution.py:438
  86.2 1.5 %collective-permute-start.16 = (bf16[128,1024]{1,0:T(8,128)(2,1)S(1)}, bf16[128,1024]{1,0:T(8,128)(2,1)S(1)}, u32[]{:S(2)}, u32[]{:S(2)}) collective-permute-start(bf16[128,1024]{1,0:T(8,128)(2,1)S(1)} %fusion.14), channel_id=1, source_target_pairs={{0,1},{1,0},{2,3},{3,2},{4,5},{5,4},{6,7},{7,6},{8,9},{9,8},{10,11... | collective-permute-start | bytes 786440 | tf_op jit(solution)/shard_map/ppermute | solution.py:441
  87.7 2.0 %fusion.11.kept1_ref = bf16[128,1024]{1,0:T(8,128)(2,1)S(1)} fusion(bf16[128,1024]{1,0:T(8,128)(2,1)S(1)} %join.1, bf16[1024,4096]{1,0:T(8,128)(2,1)} %param.13, s32[]{:T(128)S(6)} %select_n.13), kind=kOutput, calls=%fused_computation.9 | convolution fusion | flops 268566528 | bytes 2621444 | tf_op jit(solution)/shard_map/dot_general | solution.py:438
  89.7 2.0 %fusion.8.kept0_ref = bf16[128,1024]{1,0:T(8,128)(2,1)S(1)} fusion(bf16[128,1024]{1,0:T(8,128)(2,1)S(1)} %join.1, bf16[1024,4096]{1,0:T(8,128)(2,1)} %param.13, s32[]{:T(128)S(6)} %select_n.12), kind=kOutput, calls=%fused_computation.8 | convolution fusion | flops 268566528 | bytes 2621444 | tf_op jit(solution)/shard_map/dot_general | solution.py:438
  91.7 0.0 collective-permute-done.17.received1_ref
  91.8 3.7 %collective-permute-done.16.received0_ref = bf16[128,1024]{1,0:T(8,128)(2,1)S(1)} collective-permute-done((bf16[128,1024]{1,0:T(8,128)(2,1)S(1)}, bf16[128,1024]{1,0:T(8,128)(2,1)S(1)}, u32[]{:S(2)}, u32[]{:S(2)}) %collective-permute-start.16) | collective-permute-done | bytes 262176 | tf_op jit(solution)/shard_map/ppermute | solution.py:441
  95.5 0.8 add.33
  (26 shorter events, 0.1 us)
Async XLA Ops:
  0.0 5.7 %collective-permute-start = (s32[1,2,2,2]{3,2,1,0:T(2,128)}, s32[1,2,2,2]{3,2,1,0:T(2,128)S(1)}, u32[]{:S(2)}, u32[]{:S(2)}) collective-permute-start(s32[1,2,2,2]{3,2,1,0:T(2,128)} %param.11), channel_id=1, source_target_pairs={{0,2},{2,4},{4,6},{6,8},{8,10},{10,12},{12,14},{14,16},{16,18},{18... | collective-permute-start | bytes 104 | tf_op jit(solution)/shard_map/ppermute | solution.py:385
  5.7 33.7 %all-to-all-start = ((bf16[8,3,128,128]{3,2,1,0:T(8,128)(2,1)}), bf16[8,3,128,128]{3,2,1,0:T(8,128)(2,1)S(1)}, u32[]{:S(2)}, u32[]{:S(2)}) async-start(bf16[8,3,128,128]{3,2,1,0:T(8,128)(2,1)} %split_heads.1), calls=%async_computation | async-start | bytes 1572864 | tf_op jit(solution)/shard_map/all_to_all | solution.py:388
  17.5 3.0 %collective-permute-start.4 = (bf16[128,1024]{1,0:T(8,128)(2,1)}, bf16[128,1024]{1,0:T(8,128)(2,1)S(1)}, u32[]{:S(2)}, u32[]{:S(2)}) collective-permute-start(bf16[128,1024]{1,0:T(8,128)(2,1)} %bitcast.18), channel_id=1, source_target_pairs={{0,64},{64,0},{1,65},{65,1},{2,66},{66,2},{3,67},{67,3},{4,68},{68... | collective-permute-start | bytes 786440 | tf_op jit(solution)/shard_map/ppermute | solution.py:393
  17.5 9.0 %collective-permute-start.1 = (bf16[128,1024]{1,0:T(8,128)(2,1)}, bf16[128,1024]{1,0:T(8,128)(2,1)S(1)}, u32[]{:S(2)}, u32[]{:S(2)}) collective-permute-start(bf16[128,1024]{1,0:T(8,128)(2,1)} %bitcast.19), channel_id=1, source_target_pairs={{0,128},{128,0},{1,129},{129,1},{2,130},{130,2},{3,131},{131,3},{4... | collective-permute-start | bytes 786440 | tf_op jit(solution)/shard_map/ppermute | solution.py:392
  18.8 1.7 %copy-start.2 = (s32[2,2,2,2]{3,2,1,0:T(2,128)}, s32[2,2,2,2]{3,2,1,0:T(2,128)S(1)}, u32[]{:S(2)}) copy-start(s32[2,2,2,2]{3,2,1,0:T(2,128)S(1)} %constant_dynamic-update-slice_fusion.ids0_ref) | copy-start | bytes 196
  18.8 1.7 %collective-permute-start.3 = (s32[2,2,2,2]{3,2,1,0:T(2,128)S(1)}, s32[2,2,2,2]{3,2,1,0:T(2,128)S(1)}, u32[]{:S(2)}, u32[]{:S(2)}) collective-permute-start(s32[2,2,2,2]{3,2,1,0:T(2,128)S(1)} %constant_dynamic-update-slice_fusion.ids0_ref), channel_id=1, source_target_pairs={{0,64},{64,0},{1,65},{65,1},{2,66},{66,2},{3,67},{67,3},{4,68},{68... | collective-permute-start | bytes 200 | tf_op jit(solution)/shard_map/ppermute | solution.py:395
  18.9 7.6 %collective-permute-start.2 = (s32[2,2,2,2]{3,2,1,0:T(2,128)S(1)}, s32[2,2,2,2]{3,2,1,0:T(2,128)S(1)}, u32[]{:S(2)}, u32[]{:S(2)}) collective-permute-start(s32[2,2,2,2]{3,2,1,0:T(2,128)S(1)} %constant_dynamic-update-slice_fusion.ids0_ref), channel_id=1, source_target_pairs={{0,128},{128,0},{1,129},{129,1},{2,130},{130,2},{3,131},{131,3},{4... | collective-permute-start | bytes 200 | tf_op jit(solution)/shard_map/ppermute | solution.py:394
  20.5 0.6 copy-start.7
  20.5 0.7 copy-start.4
  24.9 54.6 %copy-start = (bf16[1056,128]{1,0:T(8,128)(2,1)S(1)}, bf16[1056,128]{1,0:T(8,128)(2,1)}, u32[]{:S(2)}) copy-start(bf16[1056,128]{1,0:T(8,128)(2,1)} %get-tuple-element.32.refs_0_) | copy-start | bytes 811012
  26.5 2.0 %copy-start.6 = (s32[2,2,2,2]{3,2,1,0:T(2,128)}, s32[2,2,2,2]{3,2,1,0:T(2,128)S(1)}, u32[]{:S(2)}) copy-start(s32[2,2,2,2]{3,2,1,0:T(2,128)S(1)} %collective-permute-done.2.ids0_ref) | copy-start | bytes 196
  26.5 2.0 %copy-start.3 = (bf16[128,1024]{1,0:T(8,128)(2,1)}, bf16[128,1024]{1,0:T(8,128)(2,1)S(1)}, u32[]{:S(2)}) copy-start(bf16[128,1024]{1,0:T(8,128)(2,1)S(1)} %collective-permute-done.1.q0_ref) | copy-start | bytes 786436
  26.5 2.0 %collective-permute-start.6 = (bf16[128,1024]{1,0:T(8,128)(2,1)S(1)}, bf16[128,1024]{1,0:T(8,128)(2,1)S(1)}, u32[]{:S(2)}, u32[]{:S(2)}) collective-permute-start(bf16[128,1024]{1,0:T(8,128)(2,1)S(1)} %collective-permute-done.1.q0_ref), channel_id=1, source_target_pairs={{0,64},{64,0},{1,65},{65,1},{2,66},{66,2},{3,67},{67,3},{4,68},{68... | collective-permute-start | bytes 786440 | tf_op jit(solution)/shard_map/ppermute | solution.py:400
  26.6 8.3 %collective-permute-start.7 = (bf16[1056,128]{1,0:T(8,128)(2,1)}, bf16[1056,128]{1,0:T(8,128)(2,1)S(1)}, u32[]{:S(2)}, u32[]{:S(2)}) collective-permute-start(bf16[1056,128]{1,0:T(8,128)(2,1)} %get-tuple-element.36), channel_id=1, source_target_pairs={{0,64},{64,0},{1,65},{65,1},{2,66},{66,2},{3,67},{67,3},{4,68},{68... | collective-permute-start | bytes 811016 | tf_op jit(solution)/shard_map/ppermute | solution.py:405
  27.1 1.4 %collective-permute-start.5 = (s32[2,2,2,2]{3,2,1,0:T(2,128)S(1)}, s32[2,2,2,2]{3,2,1,0:T(2,128)S(1)}, u32[]{:S(2)}, u32[]{:S(2)}) collective-permute-start(s32[2,2,2,2]{3,2,1,0:T(2,128)S(1)} %collective-permute-done.2.ids0_ref), channel_id=1, source_target_pairs={{0,64},{64,0},{1,65},{65,1},{2,66},{66,2},{3,67},{67,3},{4,68},{68... | collective-permute-start | bytes 200 | tf_op jit(solution)/shard_map/ppermute | solution.py:401
  28.5 0.6 copy-start.8
  29.1 0.7 copy-start.5
  34.8 12.0 %collective-permute-start.10 = (bf16[1056,128]{1,0:T(8,128)(2,1)}, bf16[1056,128]{1,0:T(8,128)(2,1)S(1)}, u32[]{:S(2)}, u32[]{:S(2)}) collective-permute-start(bf16[1056,128]{1,0:T(8,128)(2,1)} %get-tuple-element.38), channel_id=1, source_target_pairs={{0,64},{64,0},{1,65},{65,1},{2,66},{66,2},{3,67},{67,3},{4,68},{68... | collective-permute-start | bytes 811016 | tf_op jit(solution)/shard_map/ppermute | solution.py:406
  40.3 10.7 %collective-permute-start.8 = (bf16[4,2,128,128]{3,2,1,0:T(8,128)(2,1)}, bf16[4,2,128,128]{3,2,1,0:T(8,128)(2,1)S(1)}, u32[]{:S(2)}, u32[]{:S(2)}) collective-permute-start(bf16[4,2,128,128]{3,2,1,0:T(8,128)(2,1)} %get-tuple-element.56), channel_id=1, source_target_pairs={{0,2},{2,4},{4,6},{6,0},{1,3},{3,5},{5,7},{7,1},{8,10},{10,12},{12... | collective-permute-start | bytes 786440 | tf_op jit(solution)/shard_map/ppermute | solution.py:411
  40.3 10.7 %collective-permute-start.9 = (bf16[4,2,128,128]{3,2,1,0:T(8,128)(2,1)}, bf16[4,2,128,128]{3,2,1,0:T(8,128)(2,1)S(1)}, u32[]{:S(2)}, u32[]{:S(2)}) collective-permute-start(bf16[4,2,128,128]{3,2,1,0:T(8,128)(2,1)} %get-tuple-element.55), channel_id=1, source_target_pairs={{0,6},{2,0},{4,2},{6,4},{1,7},{3,1},{5,3},{7,5},{8,14},{10,8},{12,... | collective-permute-start | bytes 786440 | tf_op jit(solution)/shard_map/ppermute | solution.py:412
  43.5 13.3 %collective-permute-start.13 = (bf16[4,2,128,128]{3,2,1,0:T(8,128)(2,1)}, bf16[4,2,128,128]{3,2,1,0:T(8,128)(2,1)S(1)}, u32[]{:S(2)}, u32[]{:S(2)}) collective-permute-start(bf16[4,2,128,128]{3,2,1,0:T(8,128)(2,1)} %get-tuple-element.55), channel_id=1, source_target_pairs={{0,2},{2,4},{4,6},{6,0},{1,3},{3,5},{5,7},{7,1},{8,10},{10,12},{12... | collective-permute-start | bytes 786440 | tf_op jit(solution)/shard_map/ppermute | solution.py:413
  43.5 13.3 %collective-permute-start.14 = (bf16[4,2,128,128]{3,2,1,0:T(8,128)(2,1)}, bf16[4,2,128,128]{3,2,1,0:T(8,128)(2,1)S(1)}, u32[]{:S(2)}, u32[]{:S(2)}) collective-permute-start(bf16[4,2,128,128]{3,2,1,0:T(8,128)(2,1)} %get-tuple-element.56), channel_id=1, source_target_pairs={{0,6},{2,0},{4,2},{6,4},{1,7},{3,1},{5,3},{7,5},{8,14},{10,8},{12,... | collective-permute-start | bytes 786440 | tf_op jit(solution)/shard_map/ppermute | solution.py:414
  46.7 1.0 copy-start.1
  50.9 9.3 %collective-permute-start.15 = (bf16[1056,128]{1,0:T(8,128)(2,1)S(1)}, bf16[1056,128]{1,0:T(8,128)(2,1)S(1)}, u32[]{:S(2)}, u32[]{:S(2)}) collective-permute-start(bf16[1056,128]{1,0:T(8,128)(2,1)S(1)} %merge.1), channel_id=1, source_target_pairs={{0,128},{128,0},{1,129},{129,1},{2,130},{130,2},{3,131},{131,3},{4... | collective-permute-start | bytes 811016 | tf_op jit(solution)/shard_map/ppermute | solution.py:422
  51.7 8.4 %collective-permute-start.11 = (bf16[4,2,128,128]{3,2,1,0:T(8,128)(2,1)S(1)}, bf16[4,2,128,128]{3,2,1,0:T(8,128)(2,1)S(1)}, u32[]{:S(2)}, u32[]{:S(2)}) collective-permute-start(bf16[4,2,128,128]{3,2,1,0:T(8,128)(2,1)S(1)} %collective-permute-done.8.refs_0_), channel_id=1, source_target_pairs={{0,2},{2,4},{4,6},{6,0},{1,3},{3,5},{5,7},{7,1},{8,10},{10,12},{12... | collective-permute-start | bytes 786440 | tf_op jit(solution)/shard_map/ppermute | solution.py:420
  51.7 8.4 %collective-permute-start.12 = (bf16[4,2,128,128]{3,2,1,0:T(8,128)(2,1)S(1)}, bf16[4,2,128,128]{3,2,1,0:T(8,128)(2,1)S(1)}, u32[]{:S(2)}, u32[]{:S(2)}) collective-permute-start(bf16[4,2,128,128]{3,2,1,0:T(8,128)(2,1)S(1)} %collective-permute-done.9.refs_3_), channel_id=1, source_target_pairs={{0,6},{2,0},{4,2},{6,4},{1,7},{3,1},{5,3},{7,5},{8,14},{10,8},{12,... | collective-permute-start | bytes 786440 | tf_op jit(solution)/shard_map/ppermute | solution.py:421
  62.7 16.9 %all-to-all-start.1 = ((bf16[8,128,128]{2,1,0:T(8,128)(2,1)}), bf16[8,128,128]{2,1,0:T(8,128)(2,1)S(1)}, u32[]{:S(2)}, u32[]{:S(2)}) async-start(bf16[8,128,128]{2,1,0:T(8,128)(2,1)} %attend_far.1), calls=%async_computation.1 | async-start | bytes 524288 | tf_op jit(solution)/shard_map/all_to_all | solution.py:431
  81.9 9.9 %collective-permute-start.17 = (bf16[128,1024]{1,0:T(8,128)(2,1)S(1)}, bf16[128,1024]{1,0:T(8,128)(2,1)S(1)}, u32[]{:S(2)}, u32[]{:S(2)}) collective-permute-start(bf16[128,1024]{1,0:T(8,128)(2,1)S(1)} %fusion.17), channel_id=1, source_target_pairs={{0,1},{1,0},{2,3},{3,2},{4,5},{5,4},{6,7},{7,6},{8,9},{9,8},{10,11... | collective-permute-start | bytes 786440 | tf_op jit(solution)/shard_map/ppermute | solution.py:441
  86.2 9.3 %collective-permute-start.16 = (bf16[128,1024]{1,0:T(8,128)(2,1)S(1)}, bf16[128,1024]{1,0:T(8,128)(2,1)S(1)}, u32[]{:S(2)}, u32[]{:S(2)}) collective-permute-start(bf16[128,1024]{1,0:T(8,128)(2,1)S(1)} %fusion.14), channel_id=1, source_target_pairs={{0,1},{1,0},{2,3},{3,2},{4,5},{5,4},{6,7},{7,6},{8,9},{9,8},{10,11... | collective-permute-start | bytes 786440 | tf_op jit(solution)/shard_map/ppermute | solution.py:441

commit v2 on v1

--- a/solution.py
+++ b/solution.py
@@ -143,14 +143,8 @@
 
 
 def cross_kernel(ids0_ref, ids1_ref, place_ref, q0_ref, q1_ref, db_ref, out0_ref, out1_ref, *refs):
-    top, total, summed, blocks, queries, arrived, ready = refs
+    top, total, summed, blocks, ready = refs
     here = place_ref[0]
-    fetches = [
-        pltpu.make_async_copy(q_ref, queries.at[slot], arrived.at[slot])
-        for slot, q_ref in enumerate((q0_ref, q1_ref))
-    ]
-    for fetch in fetches:
-        fetch.start()
 
     def named(ids_ref, index):
         which, span, n = (index + 2) // 4, lax.rem(index // 2 + 1, 2), lax.rem(index, 2)
@@ -171,16 +165,17 @@
             return carry
 
         lax.fori_loop(0, 6, request, 0)
-    for fetch in fetches:
-        fetch.wait()
     row = lax.broadcasted_iota(jnp.int32, (1, ROWS), 1)
     group_of = (row + 1) // 64
-    for slot, ids_ref, out_ref in ((0, ids0_ref, out0_ref), (1, ids1_ref, out1_ref)):
+    for slot, ids_ref, q_ref, out_ref in (
+        (0, ids0_ref, q0_ref, out0_ref),
+        (1, ids1_ref, q1_ref, out1_ref),
+    ):
         top[...] = jnp.full(top.shape, LOW, F32)
         total[...] = jnp.zeros(total.shape, F32)
         summed[...] = jnp.zeros(summed.shape, F32)
 
-        def neighbour(index, carry, ids_ref=ids_ref, slot=slot):
+        def neighbour(index, carry, slot=slot, ids_ref=ids_ref, q_ref=q_ref):
             shard, block = named(ids_ref, index)
             place = 6 * slot + index
 
@@ -192,7 +187,7 @@
                 scores = [
                     lax.dot_general(
                         blocks[place, 0, :, c],
-                        queries[slot, :, c],
+                        q_ref[:, c],
                         (((1,), (1,)), ((), ())),
                         preferred_element_type=F32,
                     )
@@ -243,18 +238,16 @@
     return pl.pallas_call(
         cross_kernel,
         out_shape=(shape,) * 2,
-        in_specs=[SMEM] * 3 + [pl.BlockSpec(memory_space=pl.ANY)] * 3,
+        in_specs=[SMEM] * 3 + [VMEM] * 2 + [pl.BlockSpec(memory_space=pl.ANY)],
         out_specs=(VMEM,) * 2,
         scratch_shapes=[
             pltpu.VMEM((HEADS, ROWS), F32),
             pltpu.VMEM((HEADS, ROWS), F32),
             pltpu.VMEM((HEADS, HD, ROWS), F32),
             pltpu.VMEM((12, 2, RETR, HEADS * HD), BF16),
-            pltpu.VMEM((2, ROWS, HEADS * HD), BF16),
-            pltpu.SemaphoreType.DMA((2,)),
             pltpu.SemaphoreType.DMA((12,)),
         ],
-        compiler_params=params(56 * 1024 * 1024),
+        compiler_params=params(52 * 1024 * 1024),
         name="cross_attend",
         cost_estimate=pl.CostEstimate(
             flops=2_000_000_000, bytes_accessed=5_000_000, transcendentals=1_000_000
@@ -413,7 +406,7 @@
     below_high = lax.ppermute(kv_high, "y", up)
     above_low = lax.ppermute(kv_low, "y", down)
     across_part = merge(across_part, diagonal_part)
-    below_low, above_high, own, across_part = lax.optimization_barrier(
+    below_low, above_high, own, _ = lax.optimization_barrier(
         (below_low, above_high, own, across_part)
     )
 

time: 97.7 us -> 94.8 us (0.970)
  waiting for transfers between devices: 26.1 us -> 30 us
  Pallas kernels: 19.8 us -> 16.4 us
  local copies, waits for them, and re-layouts: 4.44 us -> 2.46 us
  starting transfers between devices: 37.7 us -> 36.3 us
    pallas_call x2, Pallas kernels: 8.69 us -> 5.4 us  [cross_attend(): pl.pallas_call(cross_kernel, out_shape=(shape,) * 2, in_specs=[SMEM] * 3...]
    ppermute x1, waiting for transfers between devices: 1.57 us -> 3.62 us  [per_device(): ids_across = lax.ppermute(ids, 'xl', across)]
    all_to_all x1, waiting for transfers between devices: 4.56 us -> 6.56 us  [per_device(): own = lax.all_to_all(own, 'z', 0, 0, tiled=True)]
    unnamed x19 -> x3, local copies, waits for them, and re-layouts: 2.93 us -> 0.95 us
    all_to_all x1, starting transfers between devices: 5.13 us -> 3.41 us  [per_device(): self_t = lax.all_to_all(self_t, 'z', 0, 0, tiled=True)]
  transfers between devices with their start and end apart: 20 -> 20, of which waited for: 6 -> 8; matrix products, arithmetic and copies ran while one was open for 8% -> 8% of each run, Pallas kernels for 17% -> 14%
where the time goes in v2:
time: 94.8 us; the launch traced here: 93.8 us
  starting transfers between devices  36.3 us (38%)
  waiting for transfers between devices  30 us (32%)
  Pallas kernels  16.4 us (17%)
  matrix products  8.24 us (9%)
  local copies, waits for them, and re-layouts  2.46 us (3%)
    all_to_all x1, starting transfers between devices, per_device(): own = lax.all_to_all(own, 'z', 0, 0, tiled=True)  11.8 us
    all_to_all x1, waiting for transfers between devices, per_device(): self_t = lax.all_to_all(self_t, 'z', 0, 0, tiled=True)  11 us
    dot_general x4, matrix products, projected(): return jnp.dot(attended, columns, preferred_element_type=F32).astype(BF16)  8.24 us
    pallas_call x3, Pallas kernels, attend(): pl.pallas_call(functools.partial(attend_kernel, steps, len(parts), not st...  7.59 us
    all_to_all x1, waiting for transfers between devices, per_device(): own = lax.all_to_all(own, 'z', 0, 0, tiled=True)  6.56 us
    pallas_call x2, Pallas kernels, cross_attend(): pl.pallas_call(cross_kernel, out_shape=(shape,) * 2, in_specs=[SMEM] * 3...  5.4 us
    ppermute x2, starting transfers between devices, per_device(): lax.ppermute(projected(2 * (1 - xh) + piece), 'xh', ring('xh', 1))  3.7 us
    ppermute x2, waiting for transfers between devices, per_device(): lax.ppermute(projected(2 * (1 - xh) + piece), 'xh', ring('xh', 1))  3.68 us
  transfers between devices with their start and end apart: 20, of which 8 were waited for; matrix products, arithmetic and copies ran while one was open for 8% of the time, Pallas kernels for 14%

profile of v2, /device:TPU:2, one launch (start us, length us, event | category | flops | bytes accessed | tf_op | source)
XLA Modules:
  0.0 93.8 jit_solution(10798554333902952035)
XLA Ops:
  0.0 3.5 %collective-permute-start = (s32[1,2,2,2]{3,2,1,0:T(2,128)}, s32[1,2,2,2]{3,2,1,0:T(2,128)S(1)}, u32[]{:S(2)}, u32[]{:S(2)}) collective-permute-start(s32[1,2,2,2]{3,2,1,0:T(2,128)} %param.11), channel_id=1, source_target_pairs={{0,2},{2,4},{4,6},{6,8},{8,10},{10,12},{12,14},{14,16},{16,18},{18... | collective-permute-start | bytes 104 | tf_op jit(solution)/shard_map/ppermute | solution.py:378
  3.5 2.2 %split_heads.1 = bf16[8,3,128,128]{3,2,1,0:T(8,128)(2,1)} custom-call(bf16[128,1024]{1,0:T(8,128)(2,1)} %bitcast.16, bf16[128,1024]{1,0:T(8,128)(2,1)} %bitcast.17, bf16[128,1024]{1,0:T(8,128)(2,1)} %bitcast.18), custom_call_target="tpu_custom_call" | custom-call | bytes 1572864 | tf_op jit(solution)/shard_map/split_heads/pallas_call | solution.py:44
  5.7 11.8 %all-to-all-start = ((bf16[8,3,128,128]{3,2,1,0:T(8,128)(2,1)}), bf16[8,3,128,128]{3,2,1,0:T(8,128)(2,1)S(1)}, u32[]{:S(2)}, u32[]{:S(2)}) async-start(bf16[8,3,128,128]{3,2,1,0:T(8,128)(2,1)} %split_heads.1), calls=%async_computation | async-start | bytes 1572864 | tf_op jit(solution)/shard_map/all_to_all | solution.py:381
  17.5 0.0 collective-permute-start.4
  17.5 0.6 collective-permute-start.1
  18.1 0.7 constant_dynamic-update-slice_fusion.ids0_ref
  18.8 0.1 collective-permute-start.3
  18.9 1.5 %collective-permute-start.2 = (s32[2,2,2,2]{3,2,1,0:T(2,128)S(1)}, s32[2,2,2,2]{3,2,1,0:T(2,128)S(1)}, u32[]{:S(2)}, u32[]{:S(2)}) collective-permute-start(s32[2,2,2,2]{3,2,1,0:T(2,128)S(1)} %constant_dynamic-update-slice_fusion.ids0_ref), channel_id=1, source_target_pairs={{0,128},{128,0},{1,129},{129,1},{2,130},{130,2},{3,131},{131,3},{4... | collective-permute-start | bytes 200 | tf_op jit(solution)/shard_map/ppermute | solution.py:387
  20.4 0.0 collective-permute-done.3.ids1_ref
  20.4 0.0 collective-permute-done.4.q1_ref
  20.5 0.9 %copy-done = bf16[1,128,1024]{2,1,0:T(8,128)(2,1)S(1)} copy-done((bf16[1,128,1024]{2,1,0:T(8,128)(2,1)S(1)}, bf16[1,128,1024]{2,1,0:T(8,128)(2,1)}, u32[]{:S(2)}) %copy-start) | copy-done | bytes 262168
  21.4 1.5 %cross_attend.2 = (bf16[1056,128]{1,0:T(8,128)(2,1)S(1)}, bf16[1056,128]{1,0:T(8,128)(2,1)S(1)}) custom-call(s32[2,2,2,2]{3,2,1,0:T(2,128)S(1)} %constant_dynamic-update-slice_fusion.ids0_ref, s32[2,2,2,2]{3,2,1,0:T(2,128)S(1)} %collective-permute-done.3.ids1_ref, s32[1]{0:T(128)} %bitcast.6.place_ref, bf16[128,1024]{1,0:T(8,128)(2,1)S(1)} %bitcast.15, ...), custom_call_target="tpu_custom_call" | custom-call | flops 2000000000 | bytes 5000000 | tf_op jit(solution)/shard_map/cross_attend/pallas_call | solution.py:238
  22.9 3.6 %collective-permute-done.2.ids0_ref = s32[2,2,2,2]{3,2,1,0:T(2,128)S(1)} collective-permute-done((s32[2,2,2,2]{3,2,1,0:T(2,128)S(1)}, s32[2,2,2,2]{3,2,1,0:T(2,128)S(1)}, u32[]{:S(2)}, u32[]{:S(2)}) %collective-permute-start.2) | collective-permute-done | bytes 96 | tf_op jit(solution)/shard_map/ppermute | solution.py:387
  26.5 0.0 collective-permute-done.1.q0_ref
  26.5 0.8 collective-permute-start.6
  27.3 0.1 collective-permute-start.7
  27.4 0.4 collective-permute-start.5
  27.8 1.0 %collective-permute-done.5.ids1_ref = s32[2,2,2,2]{3,2,1,0:T(2,128)S(1)} collective-permute-done((s32[2,2,2,2]{3,2,1,0:T(2,128)S(1)}, s32[2,2,2,2]{3,2,1,0:T(2,128)S(1)}, u32[]{:S(2)}, u32[]{:S(2)}) %collective-permute-start.5) | collective-permute-done | bytes 96 | tf_op jit(solution)/shard_map/ppermute | solution.py:394
  28.8 3.9 %cross_attend.3 = (bf16[1056,128]{1,0:T(8,128)(2,1)S(1)}, bf16[1056,128]{1,0:T(8,128)(2,1)S(1)}) custom-call(s32[2,2,2,2]{3,2,1,0:T(2,128)S(1)} %collective-permute-done.2.ids0_ref, s32[2,2,2,2]{3,2,1,0:T(2,128)S(1)} %collective-permute-done.5.ids1_ref, s32[1]{0:T(128)} %bitcast.6.place_ref, bf16[128,1024]{1,0:T(8,128)(2,1)S(1)} %collective-permute-done.1.q0_ref, ...), custom_call_target="tpu_custom_call" | custom-call | flops 2000000000 | bytes 5000000 | tf_op jit(solution)/shard_map/cross_attend/pallas_call | solution.py:238
  32.8 0.1 collective-permute-start.10
  32.9 0.0 collective-permute-done.7.refs_1_
  32.9 6.6 %all-to-all-done.own_ref.refs_0_ = bf16[8,3,128,128]{3,2,1,0:T(8,128)(2,1)S(1)} async-done(((bf16[8,3,128,128]{3,2,1,0:T(8,128)(2,1)}), bf16[8,3,128,128]{3,2,1,0:T(8,128)(2,1)S(1)}, u32[]{:S(2)}, u32[]{:S(2)}) %all-to-all-start) | async-done | bytes 786464 | tf_op jit(solution)/shard_map/all_to_all | solution.py:381
  39.4 0.8 fusion.24
  40.2 0.0 collective-permute-start.8
  40.3 3.2 %collective-permute-start.9 = (bf16[4,2,128,128]{3,2,1,0:T(8,128)(2,1)}, bf16[4,2,128,128]{3,2,1,0:T(8,128)(2,1)S(1)}, u32[]{:S(2)}, u32[]{:S(2)}) collective-permute-start(bf16[4,2,128,128]{3,2,1,0:T(8,128)(2,1)} %get-tuple-element.53), channel_id=1, source_target_pairs={{0,6},{2,0},{4,2},{6,4},{1,7},{3,1},{5,3},{7,5},{8,14},{10,8},{12,... | collective-permute-start | bytes 786440 | tf_op jit(solution)/shard_map/ppermute | solution.py:405
  43.5 3.2 %collective-permute-start.14 = (bf16[4,2,128,128]{3,2,1,0:T(8,128)(2,1)}, bf16[4,2,128,128]{3,2,1,0:T(8,128)(2,1)S(1)}, u32[]{:S(2)}, u32[]{:S(2)}) collective-permute-start(bf16[4,2,128,128]{3,2,1,0:T(8,128)(2,1)} %get-tuple-element.54), channel_id=1, source_target_pairs={{0,6},{2,0},{4,2},{6,4},{1,7},{3,1},{5,3},{7,5},{8,14},{10,8},{12,... | collective-permute-start | bytes 786440 | tf_op jit(solution)/shard_map/ppermute | solution.py:407
  46.7 0.0 collective-permute-done.10.second_ref
  46.7 0.1 merge.1
  46.9 0.6 collective-permute-start.15
  47.5 3.4 %collective-permute-done.8.refs_0_ = bf16[4,2,128,128]{3,2,1,0:T(8,128)(2,1)S(1)} collective-permute-done((bf16[4,2,128,128]{3,2,1,0:T(8,128)(2,1)}, bf16[4,2,128,128]{3,2,1,0:T(8,128)(2,1)S(1)}, u32[]{:S(2)}, u32[]{:S(2)}) %collective-permute-start.8) | collective-permute-done | bytes 262176 | tf_op jit(solution)/shard_map/ppermute | solution.py:404
  50.9 3.2 %collective-permute-start.12 = (bf16[4,2,128,128]{3,2,1,0:T(8,128)(2,1)S(1)}, bf16[4,2,128,128]{3,2,1,0:T(8,128)(2,1)S(1)}, u32[]{:S(2)}, u32[]{:S(2)}) collective-permute-start(bf16[4,2,128,128]{3,2,1,0:T(8,128)(2,1)S(1)} %collective-permute-done.9.refs_3_), channel_id=1, source_target_pairs={{0,6},{2,0},{4,2},{6,4},{1,7},{3,1},{5,3},{7,5},{8,14},{10,8},{12,... | collective-permute-start | bytes 786440 | tf_op jit(solution)/shard_map/ppermute | solution.py:414
  54.2 1.8 %attend_near.2 = (f32[8,128]{1,0:T(8,128)S(1)}, f32[8,128]{1,0:T(8,128)S(1)}, f32[8,128,128]{2,1,0:T(8,128)S(1)}) custom-call(s32[1]{0:T(128)} %bitcast.1.y_ref, bf16[8,3,128,128]{3,2,1,0:T(8,128)(2,1)S(1)} %all-to-all-done.own_ref.refs_0_, bf16[8,3,128,128]{3,2,1,0:T(8,128)(2,1)S(1)} %all-to-all-done.own_ref.refs_0_), custom_call_target="tpu_custom_call" | custom-call | flops 350000000 | bytes 1500000 | tf_op jit(solution)/shard_map/attend_near/pallas_call | solution.py:131
  56.0 0.6 collective-permute-done.13.refs_1_
  56.5 0.0 collective-permute-done.14.refs_2_
  56.5 3.3 %attend_near.3 = (f32[8,128]{1,0:T(8,128)S(1)}, f32[8,128]{1,0:T(8,128)S(1)}, f32[8,128,128]{2,1,0:T(8,128)S(1)}) custom-call(s32[1]{0:T(128)} %bitcast.1.y_ref, bf16[8,3,128,128]{3,2,1,0:T(8,128)(2,1)S(1)} %all-to-all-done.own_ref.refs_0_, bf16[4,2,128,128]{3,2,1,0:T(8,128)(2,1)S(1)} %collective-permute-done.8.refs_0_, ...), custom_call_target="tpu_custom_call" | custom-call | flops 700000000 | bytes 1500000 | tf_op jit(solution)/shard_map/attend_near/pallas_call | solution.py:131
  59.9 2.5 %attend_far.1 = bf16[8,128,128]{2,1,0:T(8,128)(2,1)} custom-call(s32[1]{0:T(128)} %bitcast.1.y_ref, bf16[8,3,128,128]{3,2,1,0:T(8,128)(2,1)S(1)} %all-to-all-done.own_ref.refs_0_, bf16[4,2,128,128]{3,2,1,0:T(8,128)(2,1)S(1)} %collective-permute-done.11.refs_0_, bf16[4,2,128,128]{3,2,1,0:T(8,128)(2,1)S(1)} %collective-permute-done.12.refs_1_, ...), custom_call_target="tpu_custom_call" | custom-call | flops 350000000 | bytes 1500000 | tf_op jit(solution)/shard_map/attend_far/pallas_call | solution.py:131
  62.4 3.4 %all-to-all-start.1 = ((bf16[8,128,128]{2,1,0:T(8,128)(2,1)}), bf16[8,128,128]{2,1,0:T(8,128)(2,1)S(1)}, u32[]{:S(2)}, u32[]{:S(2)}) async-start(bf16[8,128,128]{2,1,0:T(8,128)(2,1)} %attend_far.1), calls=%async_computation.1 | async-start | bytes 524288 | tf_op jit(solution)/shard_map/all_to_all | solution.py:424
  65.8 11.0 %all-to-all-done.1.self_ref = bf16[8,128,128]{2,1,0:T(8,128)(2,1)S(1)} async-done(((bf16[8,128,128]{2,1,0:T(8,128)(2,1)}), bf16[8,128,128]{2,1,0:T(8,128)(2,1)S(1)}, u32[]{:S(2)}, u32[]{:S(2)}) %all-to-all-start.1) | async-done | bytes 262176 | tf_op jit(solution)/shard_map/all_to_all | solution.py:424
  76.8 0.3 join.1
  77.1 2.1 %fusion.17 = bf16[128,1024]{1,0:T(8,128)(2,1)S(1)} fusion(bf16[128,1024]{1,0:T(8,128)(2,1)S(1)} %join.1, bf16[1024,4096]{1,0:T(8,128)(2,1)} %param.13, s32[]{:T(128)S(6)} %select_n.15), kind=kOutput, calls=%fused_computation.11 | convolution fusion | flops 268566528 | bytes 2621444 | tf_op jit(solution)/shard_map/dot_general | solution.py:431
  79.2 2.2 %collective-permute-start.17 = (bf16[128,1024]{1,0:T(8,128)(2,1)S(1)}, bf16[128,1024]{1,0:T(8,128)(2,1)S(1)}, u32[]{:S(2)}, u32[]{:S(2)}) collective-permute-start(bf16[128,1024]{1,0:T(8,128)(2,1)S(1)} %fusion.17), channel_id=1, source_target_pairs={{0,1},{1,0},{2,3},{3,2},{4,5},{5,4},{6,7},{7,6},{8,9},{9,8},{10,11... | collective-permute-start | bytes 786440 | tf_op jit(solution)/shard_map/ppermute | solution.py:434
  81.4 2.1 %fusion.14 = bf16[128,1024]{1,0:T(8,128)(2,1)S(1)} fusion(bf16[128,1024]{1,0:T(8,128)(2,1)S(1)} %join.1, bf16[1024,4096]{1,0:T(8,128)(2,1)} %param.13, s32[]{:T(128)S(6)} %select_n.14), kind=kOutput, calls=%fused_computation.10 | convolution fusion | flops 268566528 | bytes 2621444 | tf_op jit(solution)/shard_map/dot_general | solution.py:431
  83.5 1.5 %collective-permute-start.16 = (bf16[128,1024]{1,0:T(8,128)(2,1)S(1)}, bf16[128,1024]{1,0:T(8,128)(2,1)S(1)}, u32[]{:S(2)}, u32[]{:S(2)}) collective-permute-start(bf16[128,1024]{1,0:T(8,128)(2,1)S(1)} %fusion.14), channel_id=1, source_target_pairs={{0,1},{1,0},{2,3},{3,2},{4,5},{5,4},{6,7},{7,6},{8,9},{9,8},{10,11... | collective-permute-start | bytes 786440 | tf_op jit(solution)/shard_map/ppermute | solution.py:434
  85.0 2.1 %fusion.11.kept1_ref = bf16[128,1024]{1,0:T(8,128)(2,1)S(1)} fusion(bf16[128,1024]{1,0:T(8,128)(2,1)S(1)} %join.1, bf16[1024,4096]{1,0:T(8,128)(2,1)} %param.13, s32[]{:T(128)S(6)} %select_n.13), kind=kOutput, calls=%fused_computation.9 | convolution fusion | flops 268566528 | bytes 2621444 | tf_op jit(solution)/shard_map/dot_general | solution.py:431
  87.0 2.1 %fusion.8.kept0_ref = bf16[128,1024]{1,0:T(8,128)(2,1)S(1)} fusion(bf16[128,1024]{1,0:T(8,128)(2,1)S(1)} %join.1, bf16[1024,4096]{1,0:T(8,128)(2,1)} %param.13, s32[]{:T(128)S(6)} %select_n.12), kind=kOutput, calls=%fused_computation.8 | convolution fusion | flops 268566528 | bytes 2621444 | tf_op jit(solution)/shard_map/dot_general | solution.py:431
  89.1 0.5 collective-permute-done.17.received1_ref
  89.6 3.2 %collective-permute-done.16.received0_ref = bf16[128,1024]{1,0:T(8,128)(2,1)S(1)} collective-permute-done((bf16[128,1024]{1,0:T(8,128)(2,1)S(1)}, bf16[128,1024]{1,0:T(8,128)(2,1)S(1)}, u32[]{:S(2)}, u32[]{:S(2)}) %collective-permute-start.16) | collective-permute-done | bytes 262176 | tf_op jit(solution)/shard_map/ppermute | solution.py:434
  92.8 0.8 add.33
  (10 shorter events, 0.0 us)
Async XLA Ops:
  0.0 5.7 %collective-permute-start = (s32[1,2,2,2]{3,2,1,0:T(2,128)}, s32[1,2,2,2]{3,2,1,0:T(2,128)S(1)}, u32[]{:S(2)}, u32[]{:S(2)}) collective-permute-start(s32[1,2,2,2]{3,2,1,0:T(2,128)} %param.11), channel_id=1, source_target_pairs={{0,2},{2,4},{4,6},{6,8},{8,10},{10,12},{12,14},{14,16},{16,18},{18... | collective-permute-start | bytes 104 | tf_op jit(solution)/shard_map/ppermute | solution.py:378
  5.7 33.7 %all-to-all-start = ((bf16[8,3,128,128]{3,2,1,0:T(8,128)(2,1)}), bf16[8,3,128,128]{3,2,1,0:T(8,128)(2,1)S(1)}, u32[]{:S(2)}, u32[]{:S(2)}) async-start(bf16[8,3,128,128]{3,2,1,0:T(8,128)(2,1)} %split_heads.1), calls=%async_computation | async-start | bytes 1572864 | tf_op jit(solution)/shard_map/all_to_all | solution.py:381
  17.5 3.0 %collective-permute-start.4 = (bf16[128,1024]{1,0:T(8,128)(2,1)}, bf16[128,1024]{1,0:T(8,128)(2,1)S(1)}, u32[]{:S(2)}, u32[]{:S(2)}) collective-permute-start(bf16[128,1024]{1,0:T(8,128)(2,1)} %bitcast.13), channel_id=1, source_target_pairs={{0,64},{64,0},{1,65},{65,1},{2,66},{66,2},{3,67},{67,3},{4,68},{68... | collective-permute-start | bytes 786440 | tf_op jit(solution)/shard_map/ppermute | solution.py:386
  17.5 9.0 %collective-permute-start.1 = (bf16[128,1024]{1,0:T(8,128)(2,1)}, bf16[128,1024]{1,0:T(8,128)(2,1)S(1)}, u32[]{:S(2)}, u32[]{:S(2)}) collective-permute-start(bf16[128,1024]{1,0:T(8,128)(2,1)} %bitcast.14), channel_id=1, source_target_pairs={{0,128},{128,0},{1,129},{129,1},{2,130},{130,2},{3,131},{131,3},{4... | collective-permute-start | bytes 786440 | tf_op jit(solution)/shard_map/ppermute | solution.py:385
  18.8 1.7 %collective-permute-start.3 = (s32[2,2,2,2]{3,2,1,0:T(2,128)S(1)}, s32[2,2,2,2]{3,2,1,0:T(2,128)S(1)}, u32[]{:S(2)}, u32[]{:S(2)}) collective-permute-start(s32[2,2,2,2]{3,2,1,0:T(2,128)S(1)} %constant_dynamic-update-slice_fusion.ids0_ref), channel_id=1, source_target_pairs={{0,64},{64,0},{1,65},{65,1},{2,66},{66,2},{3,67},{67,3},{4,68},{68... | collective-permute-start | bytes 200 | tf_op jit(solution)/shard_map/ppermute | solution.py:388
  18.9 7.6 %collective-permute-start.2 = (s32[2,2,2,2]{3,2,1,0:T(2,128)S(1)}, s32[2,2,2,2]{3,2,1,0:T(2,128)S(1)}, u32[]{:S(2)}, u32[]{:S(2)}) collective-permute-start(s32[2,2,2,2]{3,2,1,0:T(2,128)S(1)} %constant_dynamic-update-slice_fusion.ids0_ref), channel_id=1, source_target_pairs={{0,128},{128,0},{1,129},{129,1},{2,130},{130,2},{3,131},{131,3},{4... | collective-permute-start | bytes 200 | tf_op jit(solution)/shard_map/ppermute | solution.py:387
  20.5 1.0 %copy-start = (bf16[1,128,1024]{2,1,0:T(8,128)(2,1)S(1)}, bf16[1,128,1024]{2,1,0:T(8,128)(2,1)}, u32[]{:S(2)}) copy-start(bf16[1,128,1024]{2,1,0:T(8,128)(2,1)} %param.10) | copy-start | bytes 786436
  26.5 2.3 %collective-permute-start.6 = (bf16[128,1024]{1,0:T(8,128)(2,1)S(1)}, bf16[128,1024]{1,0:T(8,128)(2,1)S(1)}, u32[]{:S(2)}, u32[]{:S(2)}) collective-permute-start(bf16[128,1024]{1,0:T(8,128)(2,1)S(1)} %collective-permute-done.1.q0_ref), channel_id=1, source_target_pairs={{0,64},{64,0},{1,65},{65,1},{2,66},{66,2},{3,67},{67,3},{4,68},{68... | collective-permute-start | bytes 786440 | tf_op jit(solution)/shard_map/ppermute | solution.py:393
  27.3 5.6 %collective-permute-start.7 = (bf16[1056,128]{1,0:T(8,128)(2,1)S(1)}, bf16[1056,128]{1,0:T(8,128)(2,1)S(1)}, u32[]{:S(2)}, u32[]{:S(2)}) collective-permute-start(bf16[1056,128]{1,0:T(8,128)(2,1)S(1)} %get-tuple-element.35), channel_id=1, source_target_pairs={{0,64},{64,0},{1,65},{65,1},{2,66},{66,2},{3,67},{67,3},{4,68},{68... | collective-permute-start | bytes 811016 | tf_op jit(solution)/shard_map/ppermute | solution.py:398
  27.4 1.5 %collective-permute-start.5 = (s32[2,2,2,2]{3,2,1,0:T(2,128)S(1)}, s32[2,2,2,2]{3,2,1,0:T(2,128)S(1)}, u32[]{:S(2)}, u32[]{:S(2)}) collective-permute-start(s32[2,2,2,2]{3,2,1,0:T(2,128)S(1)} %collective-permute-done.2.ids0_ref), channel_id=1, source_target_pairs={{0,64},{64,0},{1,65},{65,1},{2,66},{66,2},{3,67},{67,3},{4,68},{68... | collective-permute-start | bytes 200 | tf_op jit(solution)/shard_map/ppermute | solution.py:394
  32.8 14.0 %collective-permute-start.10 = (bf16[1056,128]{1,0:T(8,128)(2,1)S(1)}, bf16[1056,128]{1,0:T(8,128)(2,1)S(1)}, u32[]{:S(2)}, u32[]{:S(2)}) collective-permute-start(bf16[1056,128]{1,0:T(8,128)(2,1)S(1)} %get-tuple-element.37), channel_id=1, source_target_pairs={{0,64},{64,0},{1,65},{65,1},{2,66},{66,2},{3,67},{67,3},{4,68},{68... | collective-permute-start | bytes 811016 | tf_op jit(solution)/shard_map/ppermute | solution.py:399
  40.2 10.7 %collective-permute-start.8 = (bf16[4,2,128,128]{3,2,1,0:T(8,128)(2,1)}, bf16[4,2,128,128]{3,2,1,0:T(8,128)(2,1)S(1)}, u32[]{:S(2)}, u32[]{:S(2)}) collective-permute-start(bf16[4,2,128,128]{3,2,1,0:T(8,128)(2,1)} %get-tuple-element.54), channel_id=1, source_target_pairs={{0,2},{2,4},{4,6},{6,0},{1,3},{3,5},{5,7},{7,1},{8,10},{10,12},{12... | collective-permute-start | bytes 786440 | tf_op jit(solution)/shard_map/ppermute | solution.py:404
  40.3 10.7 %collective-permute-start.9 = (bf16[4,2,128,128]{3,2,1,0:T(8,128)(2,1)}, bf16[4,2,128,128]{3,2,1,0:T(8,128)(2,1)S(1)}, u32[]{:S(2)}, u32[]{:S(2)}) collective-permute-start(bf16[4,2,128,128]{3,2,1,0:T(8,128)(2,1)} %get-tuple-element.53), channel_id=1, source_target_pairs={{0,6},{2,0},{4,2},{6,4},{1,7},{3,1},{5,3},{7,5},{8,14},{10,8},{12,... | collective-permute-start | bytes 786440 | tf_op jit(solution)/shard_map/ppermute | solution.py:405
  43.5 13.0 %collective-permute-start.13 = (bf16[4,2,128,128]{3,2,1,0:T(8,128)(2,1)}, bf16[4,2,128,128]{3,2,1,0:T(8,128)(2,1)S(1)}, u32[]{:S(2)}, u32[]{:S(2)}) collective-permute-start(bf16[4,2,128,128]{3,2,1,0:T(8,128)(2,1)} %get-tuple-element.53), channel_id=1, source_target_pairs={{0,2},{2,4},{4,6},{6,0},{1,3},{3,5},{5,7},{7,1},{8,10},{10,12},{12... | collective-permute-start | bytes 786440 | tf_op jit(solution)/shard_map/ppermute | solution.py:406
  43.5 13.0 %collective-permute-start.14 = (bf16[4,2,128,128]{3,2,1,0:T(8,128)(2,1)}, bf16[4,2,128,128]{3,2,1,0:T(8,128)(2,1)S(1)}, u32[]{:S(2)}, u32[]{:S(2)}) collective-permute-start(bf16[4,2,128,128]{3,2,1,0:T(8,128)(2,1)} %get-tuple-element.54), channel_id=1, source_target_pairs={{0,6},{2,0},{4,2},{6,4},{1,7},{3,1},{5,3},{7,5},{8,14},{10,8},{12,... | collective-permute-start | bytes 786440 | tf_op jit(solution)/shard_map/ppermute | solution.py:407
  46.9 13.0 %collective-permute-start.15 = (bf16[1056,128]{1,0:T(8,128)(2,1)S(1)}, bf16[1056,128]{1,0:T(8,128)(2,1)S(1)}, u32[]{:S(2)}, u32[]{:S(2)}) collective-permute-start(bf16[1056,128]{1,0:T(8,128)(2,1)S(1)} %merge.1), channel_id=1, source_target_pairs={{0,128},{128,0},{1,129},{129,1},{2,130},{130,2},{3,131},{131,3},{4... | collective-permute-start | bytes 811016 | tf_op jit(solution)/shard_map/ppermute | solution.py:415
  50.9 8.9 %collective-permute-start.11 = (bf16[4,2,128,128]{3,2,1,0:T(8,128)(2,1)S(1)}, bf16[4,2,128,128]{3,2,1,0:T(8,128)(2,1)S(1)}, u32[]{:S(2)}, u32[]{:S(2)}) collective-permute-start(bf16[4,2,128,128]{3,2,1,0:T(8,128)(2,1)S(1)} %collective-permute-done.8.refs_0_), channel_id=1, source_target_pairs={{0,2},{2,4},{4,6},{6,0},{1,3},{3,5},{5,7},{7,1},{8,10},{10,12},{12... | collective-permute-start | bytes 786440 | tf_op jit(solution)/shard_map/ppermute | solution.py:413
  50.9 8.9 %collective-permute-start.12 = (bf16[4,2,128,128]{3,2,1,0:T(8,128)(2,1)S(1)}, bf16[4,2,128,128]{3,2,1,0:T(8,128)(2,1)S(1)}, u32[]{:S(2)}, u32[]{:S(2)}) collective-permute-start(bf16[4,2,128,128]{3,2,1,0:T(8,128)(2,1)S(1)} %collective-permute-done.9.refs_3_), channel_id=1, source_target_pairs={{0,6},{2,0},{4,2},{6,4},{1,7},{3,1},{5,3},{7,5},{8,14},{10,8},{12,... | collective-permute-start | bytes 786440 | tf_op jit(solution)/shard_map/ppermute | solution.py:414
  62.4 14.5 %all-to-all-start.1 = ((bf16[8,128,128]{2,1,0:T(8,128)(2,1)}), bf16[8,128,128]{2,1,0:T(8,128)(2,1)S(1)}, u32[]{:S(2)}, u32[]{:S(2)}) async-start(bf16[8,128,128]{2,1,0:T(8,128)(2,1)} %attend_far.1), calls=%async_computation.1 | async-start | bytes 524288 | tf_op jit(solution)/shard_map/all_to_all | solution.py:424
  79.2 10.4 %collective-permute-start.17 = (bf16[128,1024]{1,0:T(8,128)(2,1)S(1)}, bf16[128,1024]{1,0:T(8,128)(2,1)S(1)}, u32[]{:S(2)}, u32[]{:S(2)}) collective-permute-start(bf16[128,1024]{1,0:T(8,128)(2,1)S(1)} %fusion.17), channel_id=1, source_target_pairs={{0,1},{1,0},{2,3},{3,2},{4,5},{5,4},{6,7},{7,6},{8,9},{9,8},{10,11... | collective-permute-start | bytes 786440 | tf_op jit(solution)/shard_map/ppermute | solution.py:434
  83.5 9.3 %collective-permute-start.16 = (bf16[128,1024]{1,0:T(8,128)(2,1)S(1)}, bf16[128,1024]{1,0:T(8,128)(2,1)S(1)}, u32[]{:S(2)}, u32[]{:S(2)}) collective-permute-start(bf16[128,1024]{1,0:T(8,128)(2,1)S(1)} %fusion.14), channel_id=1, source_target_pairs={{0,1},{1,0},{2,3},{3,2},{4,5},{5,4},{6,7},{7,6},{8,9},{9,8},{10,11... | collective-permute-start | bytes 786440 | tf_op jit(solution)/shard_map/ppermute | solution.py:434

commit v3 on v2

--- a/solution.py
+++ b/solution.py
@@ -361,6 +361,40 @@
     )(*kept, *received)
 
 
+PIECE = COLS // 2
+FETCHES = 8
+
+
+def fetch_kernel(place_ref, after_ref, w_ref, out_ref, done):
+    first = pl.multiple_of(2 * (1 - place_ref[0]) * PIECE, PIECE)
+    tall = w_ref.shape[0] // FETCHES
+    copies = []
+    for part in range(FETCHES):
+        rows = slice(part * tall, (part + 1) * tall)
+        copies.append(
+            pltpu.make_async_copy(
+                w_ref.at[rows, pl.ds(first, PIECE)], out_ref.at[rows], done.at[part]
+            )
+        )
+        copies[-1].start()
+    for copy in copies:
+        copy.wait()
+
+
+def fetch(place, after, weight):
+    anywhere = pl.BlockSpec(memory_space=pl.ANY)
+    return pl.pallas_call(
+        fetch_kernel,
+        out_shape=jax.ShapeDtypeStruct((weight.shape[0], PIECE), weight.dtype),
+        in_specs=[SMEM, anywhere, anywhere],
+        out_specs=VMEM,
+        scratch_shapes=[pltpu.SemaphoreType.DMA((FETCHES,))],
+        compiler_params=params(46 * 1024 * 1024),
+        name="fetch_weights",
+        cost_estimate=pl.CostEstimate(flops=0, bytes_accessed=4_200_000, transcendentals=0),
+    )(place, after, weight)
+
+
 def ring(axis, step):
     count = lax.axis_size(axis)
     return [(i, (i + step) % count) for i in range(count)]
@@ -421,18 +455,19 @@
     )
 
     self_t = attend(y_index, own, (2,), (far_low, far_high), state, last=True)
+    xh = lax.axis_index("xh")
+    ready = fetch(xh.astype(jnp.int32).reshape(1), self_t, out_weight)
     self_t = lax.all_to_all(self_t, "z", 0, 0, tiled=True)
 
     attended = join(seq_index, self_t, (own_part, beside_part, across_part))
-    xh = lax.axis_index("xh")
 
     def projected(half):
         columns = lax.dynamic_slice_in_dim(out_weight, half * (COLS // 2), COLS // 2, axis=1)
         return jnp.dot(attended, columns, preferred_element_type=F32).astype(BF16)
 
-    received = [
-        lax.ppermute(projected(2 * (1 - xh) + piece), "xh", ring("xh", 1)) for piece in range(2)
-    ]
+    theirs = [jnp.dot(attended, ready, preferred_element_type=F32).astype(BF16)]
+    theirs.append(projected(2 * (1 - xh) + 1))
+    received = [lax.ppermute(piece, "xh", ring("xh", 1)) for piece in theirs]
     return add([projected(2 * xh + piece) for piece in range(2)], received)[None]
 
 

time: 94.8 us -> 93.8 us (0.989); the launches traced: 93.8 us -> 93.7 us
  Pallas kernels: 16.4 us -> 19 us
  matrix products: 8.24 us -> 6.63 us
  local copies, waits for them, and re-layouts: 2.46 us -> 0.85 us
  waiting for transfers between devices: 30 us -> 31 us
    dot_general x4 -> x3, matrix products: 8.24 us -> 6.17 us  [projected(): return jnp.dot(attended, columns, preferred_element_type=F32).astype(BF16)]
    pallas_call x0 -> x1, Pallas kernels: none -> 1.58 us  [fetch(): pl.pallas_call(fetch_kernel, out_shape=jax.ShapeDtypeStruct((weight.shape...]
    ppermute x1, waiting for transfers between devices: 3.62 us -> 4.96 us  [per_device(): ids_across = lax.ppermute(ids, 'xl', across)]
    all_to_all x1, waiting for transfers between devices: 11 us -> 9.69 us  [per_device(): self_t = lax.all_to_all(self_t, 'z', 0, 0, tiled=True)]
    pallas_call x3, Pallas kernels: 7.59 us -> 8.64 us  [attend(): pl.pallas_call(functools.partial(attend_kernel, steps, len(parts), not st...]
  transfers between devices with their start and end apart: 20 -> 20, of which waited for: 8 -> 7; matrix products, arithmetic and copies ran while one was open for 8% -> 7% of each run, Pallas kernels for 14% -> 16%
where the time goes in v3:
time: 93.8 us; the launch traced here: 93.7 us
  starting transfers between devices  35.9 us (38%)
  waiting for transfers between devices  31 us (33%)
  Pallas kernels  19 us (20%)
  matrix products  6.63 us (7%)
    all_to_all x1, starting transfers between devices, per_device(): own = lax.all_to_all(own, 'z', 0, 0, tiled=True)  11.8 us
    all_to_all x1, waiting for transfers between devices, per_device(): self_t = lax.all_to_all(self_t, 'z', 0, 0, tiled=True)  9.69 us
    pallas_call x3, Pallas kernels, attend(): pl.pallas_call(functools.partial(attend_kernel, steps, len(parts), not st...  8.64 us
    all_to_all x1, waiting for transfers between devices, per_device(): own = lax.all_to_all(own, 'z', 0, 0, tiled=True)  7.14 us
    dot_general x3, matrix products, projected(): return jnp.dot(attended, columns, preferred_element_type=F32).astype(BF16)  6.17 us
    pallas_call x2, Pallas kernels, cross_attend(): pl.pallas_call(cross_kernel, out_shape=(shape,) * 2, in_specs=[SMEM] * 3...  5.32 us
    ppermute x1, waiting for transfers between devices, per_device(): ids_across = lax.ppermute(ids, 'xl', across)  4.96 us
    ppermute x2, starting transfers between devices, per_device(): received = [lax.ppermute(piece, 'xh', ring('xh', 1)) for piece in theirs]  3.7 us
  transfers between devices with their start and end apart: 20, of which 7 were waited for; matrix products, arithmetic and copies ran while one was open for 7% of the time, Pallas kernels for 16%

profile of v3, /device:TPU:2, one launch (start us, length us, event | category | flops | bytes accessed | tf_op | source)
XLA Modules:
  0.0 93.7 jit_solution(16800126447182014250)
XLA Ops:
  0.0 3.6 %collective-permute-start = (s32[1,2,2,2]{3,2,1,0:T(2,128)}, s32[1,2,2,2]{3,2,1,0:T(2,128)S(1)}, u32[]{:S(2)}, u32[]{:S(2)}) collective-permute-start(s32[1,2,2,2]{3,2,1,0:T(2,128)} %param.11), channel_id=1, source_target_pairs={{0,2},{2,4},{4,6},{6,8},{8,10},{10,12},{12,14},{14,16},{16,18},{18... | collective-permute-start | bytes 104 | tf_op jit(solution)/shard_map/ppermute | solution.py:412
  3.6 2.2 %split_heads.1 = bf16[8,3,128,128]{3,2,1,0:T(8,128)(2,1)} custom-call(bf16[128,1024]{1,0:T(8,128)(2,1)} %bitcast.18, bf16[128,1024]{1,0:T(8,128)(2,1)} %bitcast.19, bf16[128,1024]{1,0:T(8,128)(2,1)} %bitcast.20), custom_call_target="tpu_custom_call" | custom-call | bytes 1572864 | tf_op jit(solution)/shard_map/split_heads/pallas_call | solution.py:44
  5.8 0.0 collective-permute-done
  5.8 11.8 %all-to-all-start = ((bf16[8,3,128,128]{3,2,1,0:T(8,128)(2,1)}), bf16[8,3,128,128]{3,2,1,0:T(8,128)(2,1)S(1)}, u32[]{:S(2)}, u32[]{:S(2)}) async-start(bf16[8,3,128,128]{3,2,1,0:T(8,128)(2,1)} %split_heads.1), calls=%async_computation | async-start | bytes 1572864 | tf_op jit(solution)/shard_map/all_to_all | solution.py:415
  17.6 0.1 collective-permute-start.4
  17.7 0.6 collective-permute-start.1
  18.3 0.2 collective-permute-start.3
  18.6 1.5 %collective-permute-start.2 = (s32[2,2,2,2]{3,2,1,0:T(2,128)S(1)}, s32[2,2,2,2]{3,2,1,0:T(2,128)S(1)}, u32[]{:S(2)}, u32[]{:S(2)}) collective-permute-start(s32[2,2,2,2]{3,2,1,0:T(2,128)S(1)} %constant_dynamic-update-slice_fusion.ids0_ref), channel_id=1, source_target_pairs={{0,128},{128,0},{1,129},{129,1},{2,130},{130,2},{3,131},{131,3},{4... | collective-permute-start | bytes 200 | tf_op jit(solution)/shard_map/ppermute | solution.py:421
  20.1 0.0 collective-permute-done.3.ids1_ref
  20.1 0.0 collective-permute-done.4.q1_ref
  20.1 1.5 %cross_attend.2 = (bf16[1056,128]{1,0:T(8,128)(2,1)S(1)}, bf16[1056,128]{1,0:T(8,128)(2,1)S(1)}) custom-call(s32[2,2,2,2]{3,2,1,0:T(2,128)S(1)} %constant_dynamic-update-slice_fusion.ids0_ref, s32[2,2,2,2]{3,2,1,0:T(2,128)S(1)} %collective-permute-done.3.ids1_ref, s32[1]{0:T(128)} %bitcast.6.place_ref, bf16[128,1024]{1,0:T(8,128)(2,1)S(1)} %bitcast.17, ...), custom_call_target="tpu_custom_call" | custom-call | flops 2000000000 | bytes 5000000 | tf_op jit(solution)/shard_map/cross_attend/pallas_call | solution.py:238
  21.6 5.0 %collective-permute-done.2.ids0_ref = s32[2,2,2,2]{3,2,1,0:T(2,128)S(1)} collective-permute-done((s32[2,2,2,2]{3,2,1,0:T(2,128)S(1)}, s32[2,2,2,2]{3,2,1,0:T(2,128)S(1)}, u32[]{:S(2)}, u32[]{:S(2)}) %collective-permute-start.2) | collective-permute-done | bytes 96 | tf_op jit(solution)/shard_map/ppermute | solution.py:421
  26.5 0.0 collective-permute-done.1.q0_ref
  26.5 0.0 collective-permute-start.6
  26.5 0.5 collective-permute-start.7
  27.0 0.0 collective-permute-start.5
  27.0 1.4 %collective-permute-done.5.ids1_ref = s32[2,2,2,2]{3,2,1,0:T(2,128)S(1)} collective-permute-done((s32[2,2,2,2]{3,2,1,0:T(2,128)S(1)}, s32[2,2,2,2]{3,2,1,0:T(2,128)S(1)}, u32[]{:S(2)}, u32[]{:S(2)}) %collective-permute-start.5) | collective-permute-done | bytes 96 | tf_op jit(solution)/shard_map/ppermute | solution.py:428
  28.5 3.9 %cross_attend.3 = (bf16[1056,128]{1,0:T(8,128)(2,1)S(1)}, bf16[1056,128]{1,0:T(8,128)(2,1)S(1)}) custom-call(s32[2,2,2,2]{3,2,1,0:T(2,128)S(1)} %collective-permute-done.2.ids0_ref, s32[2,2,2,2]{3,2,1,0:T(2,128)S(1)} %collective-permute-done.5.ids1_ref, s32[1]{0:T(128)} %bitcast.6.place_ref, bf16[128,1024]{1,0:T(8,128)(2,1)S(1)} %collective-permute-done.1.q0_ref, ...), custom_call_target="tpu_custom_call" | custom-call | flops 2000000000 | bytes 5000000 | tf_op jit(solution)/shard_map/cross_attend/pallas_call | solution.py:238
  32.3 0.1 collective-permute-start.10
  32.4 0.0 collective-permute-done.7.refs_1_
  32.4 7.1 %all-to-all-done.own_ref.refs_0_ = bf16[8,3,128,128]{3,2,1,0:T(8,128)(2,1)S(1)} async-done(((bf16[8,3,128,128]{3,2,1,0:T(8,128)(2,1)}), bf16[8,3,128,128]{3,2,1,0:T(8,128)(2,1)S(1)}, u32[]{:S(2)}, u32[]{:S(2)}) %all-to-all-start) | async-done | bytes 786464 | tf_op jit(solution)/shard_map/all_to_all | solution.py:415
  39.6 0.8 fusion.18
  40.4 3.2 %collective-permute-start.9 = (bf16[4,2,128,128]{3,2,1,0:T(8,128)(2,1)}, bf16[4,2,128,128]{3,2,1,0:T(8,128)(2,1)S(1)}, u32[]{:S(2)}, u32[]{:S(2)}) collective-permute-start(bf16[4,2,128,128]{3,2,1,0:T(8,128)(2,1)} %get-tuple-element.53), channel_id=1, source_target_pairs={{0,6},{2,0},{4,2},{6,4},{1,7},{3,1},{5,3},{7,5},{8,14},{10,8},{12,... | collective-permute-start | bytes 786440 | tf_op jit(solution)/shard_map/ppermute | solution.py:439
  43.6 0.0 collective-permute-start.13
  43.6 3.2 %collective-permute-start.14 = (bf16[4,2,128,128]{3,2,1,0:T(8,128)(2,1)}, bf16[4,2,128,128]{3,2,1,0:T(8,128)(2,1)}, u32[]{:S(2)}, u32[]{:S(2)}) collective-permute-start(bf16[4,2,128,128]{3,2,1,0:T(8,128)(2,1)} %get-tuple-element.54), channel_id=1, source_target_pairs={{0,6},{2,0},{4,2},{6,4},{1,7},{3,1},{5,3},{7,5},{8,14},{10,8},{12,... | collective-permute-start | bytes 786440 | tf_op jit(solution)/shard_map/ppermute | solution.py:441
  46.9 0.1 merge.1
  47.0 0.6 collective-permute-start.15
  47.6 3.4 %collective-permute-done.8.refs_0_ = bf16[4,2,128,128]{3,2,1,0:T(8,128)(2,1)S(1)} collective-permute-done((bf16[4,2,128,128]{3,2,1,0:T(8,128)(2,1)}, bf16[4,2,128,128]{3,2,1,0:T(8,128)(2,1)S(1)}, u32[]{:S(2)}, u32[]{:S(2)}) %collective-permute-start.8) | collective-permute-done | bytes 262176 | tf_op jit(solution)/shard_map/ppermute | solution.py:438
  51.1 0.0 collective-permute-done.9.refs_3_
  51.1 0.0 collective-permute-start.11
  51.1 3.2 %collective-permute-start.12 = (bf16[4,2,128,128]{3,2,1,0:T(8,128)(2,1)S(1)}, bf16[4,2,128,128]{3,2,1,0:T(8,128)(2,1)S(1)}, u32[]{:S(2)}, u32[]{:S(2)}) collective-permute-start(bf16[4,2,128,128]{3,2,1,0:T(8,128)(2,1)S(1)} %collective-permute-done.9.refs_3_), channel_id=1, source_target_pairs={{0,6},{2,0},{4,2},{6,4},{1,7},{3,1},{5,3},{7,5},{8,14},{10,8},{12,... | collective-permute-start | bytes 786440 | tf_op jit(solution)/shard_map/ppermute | solution.py:448
  54.3 1.8 %attend_near.2 = (f32[8,128]{1,0:T(8,128)S(1)}, f32[8,128]{1,0:T(8,128)S(1)}, f32[8,128,128]{2,1,0:T(8,128)S(1)}) custom-call(s32[1]{0:T(128)} %bitcast.1.y_ref, bf16[8,3,128,128]{3,2,1,0:T(8,128)(2,1)S(1)} %all-to-all-done.own_ref.refs_0_, bf16[8,3,128,128]{3,2,1,0:T(8,128)(2,1)S(1)} %all-to-all-done.own_ref.refs_0_), custom_call_target="tpu_custom_call" | custom-call | flops 350000000 | bytes 1500000 | tf_op jit(solution)/shard_map/attend_near/pallas_call | solution.py:131
  56.1 0.7 collective-permute-done.13.refs_1_
  56.8 0.0 collective-permute-done.14.refs_2_
  56.8 4.3 %attend_near.3 = (f32[8,128]{1,0:T(8,128)S(1)}, f32[8,128]{1,0:T(8,128)S(1)}, f32[8,128,128]{2,1,0:T(8,128)S(1)}) custom-call(s32[1]{0:T(128)} %bitcast.1.y_ref, bf16[8,3,128,128]{3,2,1,0:T(8,128)(2,1)S(1)} %all-to-all-done.own_ref.refs_0_, bf16[4,2,128,128]{3,2,1,0:T(8,128)(2,1)S(1)} %collective-permute-done.8.refs_0_, ...), custom_call_target="tpu_custom_call" | custom-call | flops 700000000 | bytes 1500000 | tf_op jit(solution)/shard_map/attend_near/pallas_call | solution.py:131
  61.2 2.5 %attend_far.1.after_ref = bf16[8,128,128]{2,1,0:T(8,128)(2,1)} custom-call(s32[1]{0:T(128)} %bitcast.1.y_ref, bf16[8,3,128,128]{3,2,1,0:T(8,128)(2,1)S(1)} %all-to-all-done.own_ref.refs_0_, bf16[4,2,128,128]{3,2,1,0:T(8,128)(2,1)S(1)} %collective-permute-done.11.refs_0_, bf16[4,2,128,128]{3,2,1,0:T(8,128)(2,1)S(1)} %collective-permute-done.12.refs_1_, ...), custom_call_target="tpu_custom_call" | custom-call | flops 350000000 | bytes 1500000 | tf_op jit(solution)/shard_map/attend_far/pallas_call | solution.py:131
  63.7 3.4 %all-to-all-start.1 = ((bf16[8,128,128]{2,1,0:T(8,128)(2,1)}), bf16[8,128,128]{2,1,0:T(8,128)(2,1)S(1)}, u32[]{:S(2)}, u32[]{:S(2)}) async-start(bf16[8,128,128]{2,1,0:T(8,128)(2,1)} %attend_far.1.after_ref), calls=%async_computation.1 | async-start | bytes 524288 | tf_op jit(solution)/shard_map/all_to_all | solution.py:460
  67.1 1.6 %fetch_weights.1 = bf16[1024,1024]{1,0:T(8,128)(2,1)S(1)} custom-call(s32[1]{0:T(128)} %bitcast.8.place_ref, bf16[8,128,128]{2,1,0:T(8,128)(2,1)} %attend_far.1.after_ref, bf16[1024,4096]{1,0:T(8,128)(2,1)} %w_ref.1), custom_call_target="tpu_custom_call" | custom-call | bytes 4200000 | tf_op jit(solution)/shard_map/fetch_weights/pallas_call | solution.py:386
  68.7 9.7 %all-to-all-done.1.self_ref = bf16[8,128,128]{2,1,0:T(8,128)(2,1)S(1)} async-done(((bf16[8,128,128]{2,1,0:T(8,128)(2,1)}), bf16[8,128,128]{2,1,0:T(8,128)(2,1)S(1)}, u32[]{:S(2)}, u32[]{:S(2)}) %all-to-all-start.1) | async-done | bytes 262176 | tf_op jit(solution)/shard_map/all_to_all | solution.py:460
  78.4 0.3 join.1
  78.7 0.5 convolution_convert_fusion
  79.1 2.2 %collective-permute-start.16 = (bf16[128,1024]{1,0:T(8,128)(2,1)S(1)}, bf16[128,1024]{1,0:T(8,128)(2,1)S(1)}, u32[]{:S(2)}, u32[]{:S(2)}) collective-permute-start(bf16[128,1024]{1,0:T(8,128)(2,1)S(1)} %convolution_convert_fusion), channel_id=1, source_target_pairs={{0,1},{1,0},{2,3},{3,2},{4,5},{5,4},{6,7},{7,6},{8,9},{9,8},{10,11... | collective-permute-start | bytes 786440 | tf_op jit(solution)/shard_map/ppermute | solution.py:470
  81.4 2.1 %fusion.12 = bf16[128,1024]{1,0:T(8,128)(2,1)S(1)} fusion(bf16[128,1024]{1,0:T(8,128)(2,1)S(1)} %join.1, bf16[1024,4096]{1,0:T(8,128)(2,1)} %w_ref.1, s32[]{:T(128)S(6)} %select_n.11), kind=kOutput, calls=%fused_computation.8 | convolution fusion | flops 268566528 | bytes 2621444 | tf_op jit(solution)/shard_map/dot_general | solution.py:466
  83.4 1.5 %collective-permute-start.17 = (bf16[128,1024]{1,0:T(8,128)(2,1)S(1)}, bf16[128,1024]{1,0:T(8,128)(2,1)S(1)}, u32[]{:S(2)}, u32[]{:S(2)}) collective-permute-start(bf16[128,1024]{1,0:T(8,128)(2,1)S(1)} %fusion.12), channel_id=1, source_target_pairs={{0,1},{1,0},{2,3},{3,2},{4,5},{5,4},{6,7},{7,6},{8,9},{9,8},{10,11... | collective-permute-start | bytes 786440 | tf_op jit(solution)/shard_map/ppermute | solution.py:470
  84.9 2.1 %fusion.9.kept1_ref = bf16[128,1024]{1,0:T(8,128)(2,1)S(1)} fusion(bf16[128,1024]{1,0:T(8,128)(2,1)S(1)} %join.1, bf16[1024,4096]{1,0:T(8,128)(2,1)} %w_ref.1, s32[]{:T(128)S(6)} %select_n.10), kind=kOutput, calls=%fused_computation.7 | convolution fusion | flops 268566528 | bytes 2621444 | tf_op jit(solution)/shard_map/dot_general | solution.py:466
  87.0 2.1 %fusion.6.kept0_ref = bf16[128,1024]{1,0:T(8,128)(2,1)S(1)} fusion(bf16[128,1024]{1,0:T(8,128)(2,1)S(1)} %join.1, bf16[1024,4096]{1,0:T(8,128)(2,1)} %w_ref.1, s32[]{:T(128)S(6)} %select_n.9), kind=kOutput, calls=%fused_computation.6 | convolution fusion | flops 268566528 | bytes 2621444 | tf_op jit(solution)/shard_map/dot_general | solution.py:466
  89.1 3.7 %collective-permute-done.17.received1_ref = bf16[128,1024]{1,0:T(8,128)(2,1)S(1)} collective-permute-done((bf16[128,1024]{1,0:T(8,128)(2,1)S(1)}, bf16[128,1024]{1,0:T(8,128)(2,1)S(1)}, u32[]{:S(2)}, u32[]{:S(2)}) %collective-permute-start.17) | collective-permute-done | bytes 262176 | tf_op jit(solution)/shard_map/ppermute | solution.py:470
  92.7 0.9 add.29
  (13 shorter events, 0.0 us)
Async XLA Ops:
  0.0 18.3 %copy-start.1 = (s32[1,2,2,2]{3,2,1,0:T(2,128)S(1)}, s32[1,2,2,2]{3,2,1,0:T(2,128)}, u32[]{:S(2)}) copy-start(s32[1,2,2,2]{3,2,1,0:T(2,128)} %param.11) | copy-start | bytes 100
  0.0 17.6 %copy-start = (bf16[1,128,1024]{2,1,0:T(8,128)(2,1)S(1)}, bf16[1,128,1024]{2,1,0:T(8,128)(2,1)}, u32[]{:S(2)}) copy-start(bf16[1,128,1024]{2,1,0:T(8,128)(2,1)} %param.10) | copy-start | bytes 786436
  0.0 5.8 %collective-permute-start = (s32[1,2,2,2]{3,2,1,0:T(2,128)}, s32[1,2,2,2]{3,2,1,0:T(2,128)S(1)}, u32[]{:S(2)}, u32[]{:S(2)}) collective-permute-start(s32[1,2,2,2]{3,2,1,0:T(2,128)} %param.11), channel_id=1, source_target_pairs={{0,2},{2,4},{4,6},{6,8},{8,10},{10,12},{12,14},{14,16},{16,18},{18... | collective-permute-start | bytes 104 | tf_op jit(solution)/shard_map/ppermute | solution.py:412
  5.8 33.7 %all-to-all-start = ((bf16[8,3,128,128]{3,2,1,0:T(8,128)(2,1)}), bf16[8,3,128,128]{3,2,1,0:T(8,128)(2,1)S(1)}, u32[]{:S(2)}, u32[]{:S(2)}) async-start(bf16[8,3,128,128]{3,2,1,0:T(8,128)(2,1)} %split_heads.1), calls=%async_computation | async-start | bytes 1572864 | tf_op jit(solution)/shard_map/all_to_all | solution.py:415
  17.6 2.5 %collective-permute-start.4 = (bf16[128,1024]{1,0:T(8,128)(2,1)S(1)}, bf16[128,1024]{1,0:T(8,128)(2,1)S(1)}, u32[]{:S(2)}, u32[]{:S(2)}) collective-permute-start(bf16[128,1024]{1,0:T(8,128)(2,1)S(1)} %bitcast.15), channel_id=1, source_target_pairs={{0,64},{64,0},{1,65},{65,1},{2,66},{66,2},{3,67},{67,3},{4,68},{68... | collective-permute-start | bytes 786440 | tf_op jit(solution)/shard_map/ppermute | solution.py:420
  17.7 8.8 %collective-permute-start.1 = (bf16[128,1024]{1,0:T(8,128)(2,1)S(1)}, bf16[128,1024]{1,0:T(8,128)(2,1)S(1)}, u32[]{:S(2)}, u32[]{:S(2)}) collective-permute-start(bf16[128,1024]{1,0:T(8,128)(2,1)S(1)} %bitcast.16), channel_id=1, source_target_pairs={{0,128},{128,0},{1,129},{129,1},{2,130},{130,2},{3,131},{131,3},{4... | collective-permute-start | bytes 786440 | tf_op jit(solution)/shard_map/ppermute | solution.py:419
  18.3 1.7 %collective-permute-start.3 = (s32[2,2,2,2]{3,2,1,0:T(2,128)S(1)}, s32[2,2,2,2]{3,2,1,0:T(2,128)S(1)}, u32[]{:S(2)}, u32[]{:S(2)}) collective-permute-start(s32[2,2,2,2]{3,2,1,0:T(2,128)S(1)} %constant_dynamic-update-slice_fusion.ids0_ref), channel_id=1, source_target_pairs={{0,64},{64,0},{1,65},{65,1},{2,66},{66,2},{3,67},{67,3},{4,68},{68... | collective-permute-start | bytes 200 | tf_op jit(solution)/shard_map/ppermute | solution.py:422
  18.6 8.0 %collective-permute-start.2 = (s32[2,2,2,2]{3,2,1,0:T(2,128)S(1)}, s32[2,2,2,2]{3,2,1,0:T(2,128)S(1)}, u32[]{:S(2)}, u32[]{:S(2)}) collective-permute-start(s32[2,2,2,2]{3,2,1,0:T(2,128)S(1)} %constant_dynamic-update-slice_fusion.ids0_ref), channel_id=1, source_target_pairs={{0,128},{128,0},{1,129},{129,1},{2,130},{130,2},{3,131},{131,3},{4... | collective-permute-start | bytes 200 | tf_op jit(solution)/shard_map/ppermute | solution.py:421
  26.5 1.9 %collective-permute-start.6 = (bf16[128,1024]{1,0:T(8,128)(2,1)S(1)}, bf16[128,1024]{1,0:T(8,128)(2,1)S(1)}, u32[]{:S(2)}, u32[]{:S(2)}) collective-permute-start(bf16[128,1024]{1,0:T(8,128)(2,1)S(1)} %collective-permute-done.1.q0_ref), channel_id=1, source_target_pairs={{0,64},{64,0},{1,65},{65,1},{2,66},{66,2},{3,67},{67,3},{4,68},{68... | collective-permute-start | bytes 786440 | tf_op jit(solution)/shard_map/ppermute | solution.py:427
  26.5 5.9 %collective-permute-start.7 = (bf16[1056,128]{1,0:T(8,128)(2,1)S(1)}, bf16[1056,128]{1,0:T(8,128)(2,1)S(1)}, u32[]{:S(2)}, u32[]{:S(2)}) collective-permute-start(bf16[1056,128]{1,0:T(8,128)(2,1)S(1)} %get-tuple-element.35), channel_id=1, source_target_pairs={{0,64},{64,0},{1,65},{65,1},{2,66},{66,2},{3,67},{67,3},{4,68},{68... | collective-permute-start | bytes 811016 | tf_op jit(solution)/shard_map/ppermute | solution.py:432
  27.0 1.4 %collective-permute-start.5 = (s32[2,2,2,2]{3,2,1,0:T(2,128)S(1)}, s32[2,2,2,2]{3,2,1,0:T(2,128)S(1)}, u32[]{:S(2)}, u32[]{:S(2)}) collective-permute-start(s32[2,2,2,2]{3,2,1,0:T(2,128)S(1)} %collective-permute-done.2.ids0_ref), channel_id=1, source_target_pairs={{0,64},{64,0},{1,65},{65,1},{2,66},{66,2},{3,67},{67,3},{4,68},{68... | collective-permute-start | bytes 200 | tf_op jit(solution)/shard_map/ppermute | solution.py:428
  32.3 14.6 %collective-permute-start.10 = (bf16[1056,128]{1,0:T(8,128)(2,1)S(1)}, bf16[1056,128]{1,0:T(8,128)(2,1)S(1)}, u32[]{:S(2)}, u32[]{:S(2)}) collective-permute-start(bf16[1056,128]{1,0:T(8,128)(2,1)S(1)} %get-tuple-element.37), channel_id=1, source_target_pairs={{0,64},{64,0},{1,65},{65,1},{2,66},{66,2},{3,67},{67,3},{4,68},{68... | collective-permute-start | bytes 811016 | tf_op jit(solution)/shard_map/ppermute | solution.py:433
  40.4 10.7 %collective-permute-start.8 = (bf16[4,2,128,128]{3,2,1,0:T(8,128)(2,1)}, bf16[4,2,128,128]{3,2,1,0:T(8,128)(2,1)S(1)}, u32[]{:S(2)}, u32[]{:S(2)}) collective-permute-start(bf16[4,2,128,128]{3,2,1,0:T(8,128)(2,1)} %get-tuple-element.54), channel_id=1, source_target_pairs={{0,2},{2,4},{4,6},{6,0},{1,3},{3,5},{5,7},{7,1},{8,10},{10,12},{12... | collective-permute-start | bytes 786440 | tf_op jit(solution)/shard_map/ppermute | solution.py:438
  40.4 10.7 %collective-permute-start.9 = (bf16[4,2,128,128]{3,2,1,0:T(8,128)(2,1)}, bf16[4,2,128,128]{3,2,1,0:T(8,128)(2,1)S(1)}, u32[]{:S(2)}, u32[]{:S(2)}) collective-permute-start(bf16[4,2,128,128]{3,2,1,0:T(8,128)(2,1)} %get-tuple-element.53), channel_id=1, source_target_pairs={{0,6},{2,0},{4,2},{6,4},{1,7},{3,1},{5,3},{7,5},{8,14},{10,8},{12,... | collective-permute-start | bytes 786440 | tf_op jit(solution)/shard_map/ppermute | solution.py:439
  43.6 13.1 %collective-permute-start.13 = (bf16[4,2,128,128]{3,2,1,0:T(8,128)(2,1)}, bf16[4,2,128,128]{3,2,1,0:T(8,128)(2,1)}, u32[]{:S(2)}, u32[]{:S(2)}) collective-permute-start(bf16[4,2,128,128]{3,2,1,0:T(8,128)(2,1)} %get-tuple-element.53), channel_id=1, source_target_pairs={{0,2},{2,4},{4,6},{6,0},{1,3},{3,5},{5,7},{7,1},{8,10},{10,12},{12... | collective-permute-start | bytes 786440 | tf_op jit(solution)/shard_map/ppermute | solution.py:440
  43.6 13.1 %collective-permute-start.14 = (bf16[4,2,128,128]{3,2,1,0:T(8,128)(2,1)}, bf16[4,2,128,128]{3,2,1,0:T(8,128)(2,1)}, u32[]{:S(2)}, u32[]{:S(2)}) collective-permute-start(bf16[4,2,128,128]{3,2,1,0:T(8,128)(2,1)} %get-tuple-element.54), channel_id=1, source_target_pairs={{0,6},{2,0},{4,2},{6,4},{1,7},{3,1},{5,3},{7,5},{8,14},{10,8},{12,... | collective-permute-start | bytes 786440 | tf_op jit(solution)/shard_map/ppermute | solution.py:441
  47.0 14.1 %collective-permute-start.15 = (bf16[1056,128]{1,0:T(8,128)(2,1)S(1)}, bf16[1056,128]{1,0:T(8,128)(2,1)S(1)}, u32[]{:S(2)}, u32[]{:S(2)}) collective-permute-start(bf16[1056,128]{1,0:T(8,128)(2,1)S(1)} %merge.1), channel_id=1, source_target_pairs={{0,128},{128,0},{1,129},{129,1},{2,130},{130,2},{3,131},{131,3},{4... | collective-permute-start | bytes 811016 | tf_op jit(solution)/shard_map/ppermute | solution.py:449
  51.1 10.1 %collective-permute-start.11 = (bf16[4,2,128,128]{3,2,1,0:T(8,128)(2,1)S(1)}, bf16[4,2,128,128]{3,2,1,0:T(8,128)(2,1)S(1)}, u32[]{:S(2)}, u32[]{:S(2)}) collective-permute-start(bf16[4,2,128,128]{3,2,1,0:T(8,128)(2,1)S(1)} %collective-permute-done.8.refs_0_), channel_id=1, source_target_pairs={{0,2},{2,4},{4,6},{6,0},{1,3},{3,5},{5,7},{7,1},{8,10},{10,12},{12... | collective-permute-start | bytes 786440 | tf_op jit(solution)/shard_map/ppermute | solution.py:447
  51.1 10.1 %collective-permute-start.12 = (bf16[4,2,128,128]{3,2,1,0:T(8,128)(2,1)S(1)}, bf16[4,2,128,128]{3,2,1,0:T(8,128)(2,1)S(1)}, u32[]{:S(2)}, u32[]{:S(2)}) collective-permute-start(bf16[4,2,128,128]{3,2,1,0:T(8,128)(2,1)S(1)} %collective-permute-done.9.refs_3_), channel_id=1, source_target_pairs={{0,6},{2,0},{4,2},{6,4},{1,7},{3,1},{5,3},{7,5},{8,14},{10,8},{12,... | collective-permute-start | bytes 786440 | tf_op jit(solution)/shard_map/ppermute | solution.py:448
  63.7 14.7 %all-to-all-start.1 = ((bf16[8,128,128]{2,1,0:T(8,128)(2,1)}), bf16[8,128,128]{2,1,0:T(8,128)(2,1)S(1)}, u32[]{:S(2)}, u32[]{:S(2)}) async-start(bf16[8,128,128]{2,1,0:T(8,128)(2,1)} %attend_far.1.after_ref), calls=%async_computation.1 | async-start | bytes 524288 | tf_op jit(solution)/shard_map/all_to_all | solution.py:460
  79.1 9.9 %collective-permute-start.16 = (bf16[128,1024]{1,0:T(8,128)(2,1)S(1)}, bf16[128,1024]{1,0:T(8,128)(2,1)S(1)}, u32[]{:S(2)}, u32[]{:S(2)}) collective-permute-start(bf16[128,1024]{1,0:T(8,128)(2,1)S(1)} %convolution_convert_fusion), channel_id=1, source_target_pairs={{0,1},{1,0},{2,3},{3,2},{4,5},{5,4},{6,7},{7,6},{8,9},{9,8},{10,11... | collective-permute-start | bytes 786440 | tf_op jit(solution)/shard_map/ppermute | solution.py:470
  83.4 9.3 %collective-permute-start.17 = (bf16[128,1024]{1,0:T(8,128)(2,1)S(1)}, bf16[128,1024]{1,0:T(8,128)(2,1)S(1)}, u32[]{:S(2)}, u32[]{:S(2)}) collective-permute-start(bf16[128,1024]{1,0:T(8,128)(2,1)S(1)} %fusion.12), channel_id=1, source_target_pairs={{0,1},{1,0},{2,3},{3,2},{4,5},{5,4},{6,7},{7,6},{8,9},{9,8},{10,11... | collective-permute-start | bytes 786440 | tf_op jit(solution)/shard_map/ppermute | solution.py:470

commit v4 on v3

--- a/solution.py
+++ b/solution.py
@@ -420,12 +420,14 @@
     from_beside = lax.ppermute(mine, "core", beside)
     ids_across = lax.ppermute(ids, "xl", across)
     ids_beside = lax.ppermute(ids, "core", beside)
+    ids_diagonal = lax.ppermute(ids, dp, [(i, 3 - i) for i in range(4)])
     own_part, beside_part = cross_attend(
         place_dp, (ids, ids_beside), (mine, from_beside), database[0]
     )
-    from_across, ids_across, _ = lax.optimization_barrier((from_across, ids_across, own_part))
+    from_across, ids_across, ids_diagonal, _ = lax.optimization_barrier(
+        (from_across, ids_across, ids_diagonal, own_part)
+    )
     from_diagonal = lax.ppermute(from_across, "core", beside)
-    ids_diagonal = lax.ppermute(ids_across, "core", beside)
     across_part, diagonal_part = cross_attend(
         place_dp, (ids_across, ids_diagonal), (from_across, from_diagonal), database[0]
     )

time: 93.8 us -> 92.9 us (level)
  waiting for transfers between devices: 31 us -> 27.6 us
  Pallas kernels: 19 us -> 20.4 us
    ppermute x1, waiting for transfers between devices: 4.96 us -> 3.48 us  [per_device(): ids_across = lax.ppermute(ids, 'xl', across)]
    ppermute x1, waiting for transfers between devices: 1.41 us -> 0.01 us  [per_device(): ids_diagonal = lax.ppermute(ids, dp, [(i, 3 - i) for i in range(4)])]
    pallas_call x2, Pallas kernels: 5.32 us -> 6.73 us  [cross_attend(): pl.pallas_call(cross_kernel, out_shape=(shape,) * 2, in_specs=[SMEM] * 3...]
    ppermute x1, waiting for transfers between devices: 0.01 us -> 1.02 us  [per_device(): from_diagonal = lax.ppermute(from_across, 'core', beside)]
  transfers between devices with their start and end apart: 20 -> 20, of which waited for: 7 -> 8; matrix products, arithmetic and copies ran while one was open for 7% -> 8% of each run, Pallas kernels for 16% -> 18%
where the time goes in v4:
time: 92.9 us; the launch traced here: 91.9 us
  starting transfers between devices  36.1 us (39%)
  waiting for transfers between devices  27.6 us (30%)
  Pallas kernels  20.4 us (22%)
  matrix products  6.63 us (7%)
    all_to_all x1, starting transfers between devices, per_device(): own = lax.all_to_all(own, 'z', 0, 0, tiled=True)  11.8 us
    all_to_all x1, waiting for transfers between devices, per_device(): self_t = lax.all_to_all(self_t, 'z', 0, 0, tiled=True)  8.78 us
    pallas_call x3, Pallas kernels, attend(): pl.pallas_call(functools.partial(attend_kernel, steps, len(parts), not st...  8.59 us
    all_to_all x1, waiting for transfers between devices, per_device(): own = lax.all_to_all(own, 'z', 0, 0, tiled=True)  7.4 us
    pallas_call x2, Pallas kernels, cross_attend(): pl.pallas_call(cross_kernel, out_shape=(shape,) * 2, in_specs=[SMEM] * 3...  6.73 us
    dot_general x3, matrix products, projected(): return jnp.dot(attended, columns, preferred_element_type=F32).astype(BF16)  6.17 us
    ppermute x2, starting transfers between devices, per_device(): received = [lax.ppermute(piece, 'xh', ring('xh', 1)) for piece in theirs]  3.7 us
    ppermute x1, starting transfers between devices, per_device(): lax.ppermute(neighbour_ids, seq, [(i, i + 1) for i in range(ZS * YS - 1)])  3.6 us
  transfers between devices with their start and end apart: 20, of which 8 were waited for; matrix products, arithmetic and copies ran while one was open for 8% of the time, Pallas kernels for 18%

profile of v4, /device:TPU:2, one launch (start us, length us, event | category | flops | bytes accessed | tf_op | source)
XLA Modules:
  0.0 91.9 jit_solution(2492561316957740255)
XLA Ops:
  0.0 3.6 %collective-permute-start = (s32[1,2,2,2]{3,2,1,0:T(2,128)}, s32[1,2,2,2]{3,2,1,0:T(2,128)S(1)}, u32[]{:S(2)}, u32[]{:S(2)}) collective-permute-start(s32[1,2,2,2]{3,2,1,0:T(2,128)} %param.11), channel_id=1, source_target_pairs={{0,2},{2,4},{4,6},{6,8},{8,10},{10,12},{12,14},{14,16},{16,18},{18... | collective-permute-start | bytes 104 | tf_op jit(solution)/shard_map/ppermute | solution.py:412
  3.6 2.2 %split_heads.1 = bf16[8,3,128,128]{3,2,1,0:T(8,128)(2,1)} custom-call(bf16[128,1024]{1,0:T(8,128)(2,1)} %bitcast.18, bf16[128,1024]{1,0:T(8,128)(2,1)} %bitcast.19, bf16[128,1024]{1,0:T(8,128)(2,1)} %bitcast.20), custom_call_target="tpu_custom_call" | custom-call | bytes 1572864 | tf_op jit(solution)/shard_map/split_heads/pallas_call | solution.py:44
  5.8 11.8 %all-to-all-start = ((bf16[8,3,128,128]{3,2,1,0:T(8,128)(2,1)}), bf16[8,3,128,128]{3,2,1,0:T(8,128)(2,1)S(1)}, u32[]{:S(2)}, u32[]{:S(2)}) async-start(bf16[8,3,128,128]{3,2,1,0:T(8,128)(2,1)} %split_heads.1), calls=%async_computation | async-start | bytes 1572864 | tf_op jit(solution)/shard_map/all_to_all | solution.py:415
  17.6 0.1 collective-permute-start.5
  17.7 0.6 collective-permute-start.1
  18.3 0.2 collective-permute-start.4
  18.6 1.5 %collective-permute-start.2 = (s32[2,2,2,2]{3,2,1,0:T(2,128)S(1)}, s32[2,2,2,2]{3,2,1,0:T(2,128)S(1)}, u32[]{:S(2)}, u32[]{:S(2)}) collective-permute-start(s32[2,2,2,2]{3,2,1,0:T(2,128)S(1)} %constant_dynamic-update-slice_fusion.ids0_ref), channel_id=1, source_target_pairs={{0,128},{128,0},{1,129},{129,1},{2,130},{130,2},{3,131},{131,3},{4... | collective-permute-start | bytes 200 | tf_op jit(solution)/shard_map/ppermute | solution.py:421
  20.1 0.2 collective-permute-start.3
  20.3 0.0 collective-permute-done.4.ids1_ref
  20.3 0.0 collective-permute-done.5.q1_ref
  20.3 2.8 %cross_attend.2 = (bf16[1056,128]{1,0:T(8,128)(2,1)S(1)}, bf16[1056,128]{1,0:T(8,128)(2,1)S(1)}) custom-call(s32[2,2,2,2]{3,2,1,0:T(2,128)S(1)} %constant_dynamic-update-slice_fusion.ids0_ref, s32[2,2,2,2]{3,2,1,0:T(2,128)S(1)} %collective-permute-done.4.ids1_ref, s32[1]{0:T(128)} %bitcast.6.place_ref, bf16[128,1024]{1,0:T(8,128)(2,1)S(1)} %bitcast.17, ...), custom_call_target="tpu_custom_call" | custom-call | flops 2000000000 | bytes 5000000 | tf_op jit(solution)/shard_map/cross_attend/pallas_call | solution.py:238
  23.1 3.5 %collective-permute-done.2.ids0_ref = s32[2,2,2,2]{3,2,1,0:T(2,128)S(1)} collective-permute-done((s32[2,2,2,2]{3,2,1,0:T(2,128)S(1)}, s32[2,2,2,2]{3,2,1,0:T(2,128)S(1)}, u32[]{:S(2)}, u32[]{:S(2)}) %collective-permute-start.2) | collective-permute-done | bytes 96 | tf_op jit(solution)/shard_map/ppermute | solution.py:421
  26.6 0.0 collective-permute-done.3.ids1_ref
  26.6 0.0 collective-permute-done.1.q0_ref
  26.6 0.2 collective-permute-start.6
  26.7 0.4 collective-permute-start.7
  27.1 1.0 %collective-permute-done.6.q1_ref = bf16[128,1024]{1,0:T(8,128)(2,1)S(1)} collective-permute-done((bf16[128,1024]{1,0:T(8,128)(2,1)S(1)}, bf16[128,1024]{1,0:T(8,128)(2,1)S(1)}, u32[]{:S(2)}, u32[]{:S(2)}) %collective-permute-start.6) | collective-permute-done | bytes 262176 | tf_op jit(solution)/shard_map/ppermute | solution.py:430
  28.1 3.9 %cross_attend.3 = (bf16[1056,128]{1,0:T(8,128)(2,1)S(1)}, bf16[1056,128]{1,0:T(8,128)(2,1)S(1)}) custom-call(s32[2,2,2,2]{3,2,1,0:T(2,128)S(1)} %collective-permute-done.2.ids0_ref, s32[2,2,2,2]{3,2,1,0:T(2,128)S(1)} %collective-permute-done.3.ids1_ref, s32[1]{0:T(128)} %bitcast.6.place_ref, bf16[128,1024]{1,0:T(8,128)(2,1)S(1)} %collective-permute-done.1.q0_ref, ...), custom_call_target="tpu_custom_call" | custom-call | flops 2000000000 | bytes 5000000 | tf_op jit(solution)/shard_map/cross_attend/pallas_call | solution.py:238
  32.1 0.1 collective-permute-start.10
  32.2 7.4 %all-to-all-done.own_ref.refs_0_ = bf16[8,3,128,128]{3,2,1,0:T(8,128)(2,1)S(1)} async-done(((bf16[8,3,128,128]{3,2,1,0:T(8,128)(2,1)}), bf16[8,3,128,128]{3,2,1,0:T(8,128)(2,1)S(1)}, u32[]{:S(2)}, u32[]{:S(2)}) %all-to-all-start) | async-done | bytes 786464 | tf_op jit(solution)/shard_map/all_to_all | solution.py:415
  39.6 0.8 fusion.18
  40.4 3.2 %collective-permute-start.9 = (bf16[4,2,128,128]{3,2,1,0:T(8,128)(2,1)}, bf16[4,2,128,128]{3,2,1,0:T(8,128)(2,1)S(1)}, u32[]{:S(2)}, u32[]{:S(2)}) collective-permute-start(bf16[4,2,128,128]{3,2,1,0:T(8,128)(2,1)} %get-tuple-element.55), channel_id=1, source_target_pairs={{0,6},{2,0},{4,2},{6,4},{1,7},{3,1},{5,3},{7,5},{8,14},{10,8},{12,... | collective-permute-start | bytes 786440 | tf_op jit(solution)/shard_map/ppermute | solution.py:441
  43.6 0.0 collective-permute-start.13
  43.6 3.2 %collective-permute-start.14 = (bf16[4,2,128,128]{3,2,1,0:T(8,128)(2,1)}, bf16[4,2,128,128]{3,2,1,0:T(8,128)(2,1)}, u32[]{:S(2)}, u32[]{:S(2)}) collective-permute-start(bf16[4,2,128,128]{3,2,1,0:T(8,128)(2,1)} %get-tuple-element.56), channel_id=1, source_target_pairs={{0,6},{2,0},{4,2},{6,4},{1,7},{3,1},{5,3},{7,5},{8,14},{10,8},{12,... | collective-permute-start | bytes 786440 | tf_op jit(solution)/shard_map/ppermute | solution.py:443
  46.9 0.0 collective-permute-done.10.second_ref
  46.9 0.1 merge.1
  47.0 0.6 collective-permute-start.15
  47.6 3.4 %collective-permute-done.8.refs_0_ = bf16[4,2,128,128]{3,2,1,0:T(8,128)(2,1)S(1)} collective-permute-done((bf16[4,2,128,128]{3,2,1,0:T(8,128)(2,1)}, bf16[4,2,128,128]{3,2,1,0:T(8,128)(2,1)S(1)}, u32[]{:S(2)}, u32[]{:S(2)}) %collective-permute-start.8) | collective-permute-done | bytes 262176 | tf_op jit(solution)/shard_map/ppermute | solution.py:440
  51.1 0.0 collective-permute-done.9.refs_3_
  51.1 0.0 collective-permute-start.11
  51.1 3.2 %collective-permute-start.12 = (bf16[4,2,128,128]{3,2,1,0:T(8,128)(2,1)S(1)}, bf16[4,2,128,128]{3,2,1,0:T(8,128)(2,1)S(1)}, u32[]{:S(2)}, u32[]{:S(2)}) collective-permute-start(bf16[4,2,128,128]{3,2,1,0:T(8,128)(2,1)S(1)} %collective-permute-done.9.refs_3_), channel_id=1, source_target_pairs={{0,6},{2,0},{4,2},{6,4},{1,7},{3,1},{5,3},{7,5},{8,14},{10,8},{12,... | collective-permute-start | bytes 786440 | tf_op jit(solution)/shard_map/ppermute | solution.py:450
  54.3 1.8 %attend_near.2 = (f32[8,128]{1,0:T(8,128)S(1)}, f32[8,128]{1,0:T(8,128)S(1)}, f32[8,128,128]{2,1,0:T(8,128)S(1)}) custom-call(s32[1]{0:T(128)} %bitcast.1.y_ref, bf16[8,3,128,128]{3,2,1,0:T(8,128)(2,1)S(1)} %all-to-all-done.own_ref.refs_0_, bf16[8,3,128,128]{3,2,1,0:T(8,128)(2,1)S(1)} %all-to-all-done.own_ref.refs_0_), custom_call_target="tpu_custom_call" | custom-call | flops 350000000 | bytes 1500000 | tf_op jit(solution)/shard_map/attend_near/pallas_call | solution.py:131
  56.1 0.6 collective-permute-done.13.refs_1_
  56.7 4.3 %attend_near.3 = (f32[8,128]{1,0:T(8,128)S(1)}, f32[8,128]{1,0:T(8,128)S(1)}, f32[8,128,128]{2,1,0:T(8,128)S(1)}) custom-call(s32[1]{0:T(128)} %bitcast.1.y_ref, bf16[8,3,128,128]{3,2,1,0:T(8,128)(2,1)S(1)} %all-to-all-done.own_ref.refs_0_, bf16[4,2,128,128]{3,2,1,0:T(8,128)(2,1)S(1)} %collective-permute-done.8.refs_0_, ...), custom_call_target="tpu_custom_call" | custom-call | flops 700000000 | bytes 1500000 | tf_op jit(solution)/shard_map/attend_near/pallas_call | solution.py:131
  61.0 2.5 %attend_far.1.after_ref = bf16[8,128,128]{2,1,0:T(8,128)(2,1)} custom-call(s32[1]{0:T(128)} %bitcast.1.y_ref, bf16[8,3,128,128]{3,2,1,0:T(8,128)(2,1)S(1)} %all-to-all-done.own_ref.refs_0_, bf16[4,2,128,128]{3,2,1,0:T(8,128)(2,1)S(1)} %collective-permute-done.11.refs_0_, bf16[4,2,128,128]{3,2,1,0:T(8,128)(2,1)S(1)} %collective-permute-done.12.refs_1_, ...), custom_call_target="tpu_custom_call" | custom-call | flops 350000000 | bytes 1500000 | tf_op jit(solution)/shard_map/attend_far/pallas_call | solution.py:131
  63.5 3.4 %all-to-all-start.1 = ((bf16[8,128,128]{2,1,0:T(8,128)(2,1)}), bf16[8,128,128]{2,1,0:T(8,128)(2,1)S(1)}, u32[]{:S(2)}, u32[]{:S(2)}) async-start(bf16[8,128,128]{2,1,0:T(8,128)(2,1)} %attend_far.1.after_ref), calls=%async_computation.1 | async-start | bytes 524288 | tf_op jit(solution)/shard_map/all_to_all | solution.py:462
  67.0 1.6 %fetch_weights.1 = bf16[1024,1024]{1,0:T(8,128)(2,1)S(1)} custom-call(s32[1]{0:T(128)} %bitcast.8.place_ref, bf16[8,128,128]{2,1,0:T(8,128)(2,1)} %attend_far.1.after_ref, bf16[1024,4096]{1,0:T(8,128)(2,1)} %w_ref.1), custom_call_target="tpu_custom_call" | custom-call | bytes 4200000 | tf_op jit(solution)/shard_map/fetch_weights/pallas_call | solution.py:386
  68.5 8.8 %all-to-all-done.1.self_ref = bf16[8,128,128]{2,1,0:T(8,128)(2,1)S(1)} async-done(((bf16[8,128,128]{2,1,0:T(8,128)(2,1)}), bf16[8,128,128]{2,1,0:T(8,128)(2,1)S(1)}, u32[]{:S(2)}, u32[]{:S(2)}) %all-to-all-start.1) | async-done | bytes 262176 | tf_op jit(solution)/shard_map/all_to_all | solution.py:462
  77.3 0.3 join.1
  77.6 0.5 convolution_convert_fusion
  78.1 2.2 %collective-permute-start.16 = (bf16[128,1024]{1,0:T(8,128)(2,1)S(1)}, bf16[128,1024]{1,0:T(8,128)(2,1)S(1)}, u32[]{:S(2)}, u32[]{:S(2)}) collective-permute-start(bf16[128,1024]{1,0:T(8,128)(2,1)S(1)} %convolution_convert_fusion), channel_id=1, source_target_pairs={{0,1},{1,0},{2,3},{3,2},{4,5},{5,4},{6,7},{7,6},{8,9},{9,8},{10,11... | collective-permute-start | bytes 786440 | tf_op jit(solution)/shard_map/ppermute | solution.py:472
  80.3 2.1 %fusion.12 = bf16[128,1024]{1,0:T(8,128)(2,1)S(1)} fusion(bf16[128,1024]{1,0:T(8,128)(2,1)S(1)} %join.1, bf16[1024,4096]{1,0:T(8,128)(2,1)} %w_ref.1, s32[]{:T(128)S(6)} %select_n.11), kind=kOutput, calls=%fused_computation.8 | convolution fusion | flops 268566528 | bytes 2621444 | tf_op jit(solution)/shard_map/dot_general | solution.py:468
  82.4 1.5 %collective-permute-start.17 = (bf16[128,1024]{1,0:T(8,128)(2,1)S(1)}, bf16[128,1024]{1,0:T(8,128)(2,1)S(1)}, u32[]{:S(2)}, u32[]{:S(2)}) collective-permute-start(bf16[128,1024]{1,0:T(8,128)(2,1)S(1)} %fusion.12), channel_id=1, source_target_pairs={{0,1},{1,0},{2,3},{3,2},{4,5},{5,4},{6,7},{7,6},{8,9},{9,8},{10,11... | collective-permute-start | bytes 786440 | tf_op jit(solution)/shard_map/ppermute | solution.py:472
  83.8 2.1 %fusion.9.kept1_ref = bf16[128,1024]{1,0:T(8,128)(2,1)S(1)} fusion(bf16[128,1024]{1,0:T(8,128)(2,1)S(1)} %join.1, bf16[1024,4096]{1,0:T(8,128)(2,1)} %w_ref.1, s32[]{:T(128)S(6)} %select_n.10), kind=kOutput, calls=%fused_computation.7 | convolution fusion | flops 268566528 | bytes 2621444 | tf_op jit(solution)/shard_map/dot_general | solution.py:468
  85.9 2.1 %fusion.6.kept0_ref = bf16[128,1024]{1,0:T(8,128)(2,1)S(1)} fusion(bf16[128,1024]{1,0:T(8,128)(2,1)S(1)} %join.1, bf16[1024,4096]{1,0:T(8,128)(2,1)} %w_ref.1, s32[]{:T(128)S(6)} %select_n.9), kind=kOutput, calls=%fused_computation.6 | convolution fusion | flops 268566528 | bytes 2621444 | tf_op jit(solution)/shard_map/dot_general | solution.py:468
  88.0 0.1 collective-permute-done.16.received0_ref
  88.1 2.8 %collective-permute-done.17.received1_ref = bf16[128,1024]{1,0:T(8,128)(2,1)S(1)} collective-permute-done((bf16[128,1024]{1,0:T(8,128)(2,1)S(1)}, bf16[128,1024]{1,0:T(8,128)(2,1)S(1)}, u32[]{:S(2)}, u32[]{:S(2)}) %collective-permute-start.17) | collective-permute-done | bytes 262176 | tf_op jit(solution)/shard_map/ppermute | solution.py:472
  90.9 0.9 add.29
  (13 shorter events, 0.0 us)
Async XLA Ops:
  0.0 18.3 %copy-start.1 = (s32[1,2,2,2]{3,2,1,0:T(2,128)S(1)}, s32[1,2,2,2]{3,2,1,0:T(2,128)}, u32[]{:S(2)}) copy-start(s32[1,2,2,2]{3,2,1,0:T(2,128)} %param.11) | copy-start | bytes 100
  0.0 17.6 %copy-start = (bf16[1,128,1024]{2,1,0:T(8,128)(2,1)S(1)}, bf16[1,128,1024]{2,1,0:T(8,128)(2,1)}, u32[]{:S(2)}) copy-start(bf16[1,128,1024]{2,1,0:T(8,128)(2,1)} %param.10) | copy-start | bytes 786436
  0.0 5.8 %collective-permute-start = (s32[1,2,2,2]{3,2,1,0:T(2,128)}, s32[1,2,2,2]{3,2,1,0:T(2,128)S(1)}, u32[]{:S(2)}, u32[]{:S(2)}) collective-permute-start(s32[1,2,2,2]{3,2,1,0:T(2,128)} %param.11), channel_id=1, source_target_pairs={{0,2},{2,4},{4,6},{6,8},{8,10},{10,12},{12,14},{14,16},{16,18},{18... | collective-permute-start | bytes 104 | tf_op jit(solution)/shard_map/ppermute | solution.py:412
  5.8 33.7 %all-to-all-start = ((bf16[8,3,128,128]{3,2,1,0:T(8,128)(2,1)}), bf16[8,3,128,128]{3,2,1,0:T(8,128)(2,1)S(1)}, u32[]{:S(2)}, u32[]{:S(2)}) async-start(bf16[8,3,128,128]{3,2,1,0:T(8,128)(2,1)} %split_heads.1), calls=%async_computation | async-start | bytes 1572864 | tf_op jit(solution)/shard_map/all_to_all | solution.py:415
  17.6 2.7 %collective-permute-start.5 = (bf16[128,1024]{1,0:T(8,128)(2,1)S(1)}, bf16[128,1024]{1,0:T(8,128)(2,1)S(1)}, u32[]{:S(2)}, u32[]{:S(2)}) collective-permute-start(bf16[128,1024]{1,0:T(8,128)(2,1)S(1)} %bitcast.15), channel_id=1, source_target_pairs={{0,64},{64,0},{1,65},{65,1},{2,66},{66,2},{3,67},{67,3},{4,68},{68... | collective-permute-start | bytes 786440 | tf_op jit(solution)/shard_map/ppermute | solution.py:420
  17.7 8.9 %collective-permute-start.1 = (bf16[128,1024]{1,0:T(8,128)(2,1)S(1)}, bf16[128,1024]{1,0:T(8,128)(2,1)S(1)}, u32[]{:S(2)}, u32[]{:S(2)}) collective-permute-start(bf16[128,1024]{1,0:T(8,128)(2,1)S(1)} %bitcast.16), channel_id=1, source_target_pairs={{0,128},{128,0},{1,129},{129,1},{2,130},{130,2},{3,131},{131,3},{4... | collective-permute-start | bytes 786440 | tf_op jit(solution)/shard_map/ppermute | solution.py:419
  18.3 1.9 %collective-permute-start.4 = (s32[2,2,2,2]{3,2,1,0:T(2,128)S(1)}, s32[2,2,2,2]{3,2,1,0:T(2,128)S(1)}, u32[]{:S(2)}, u32[]{:S(2)}) collective-permute-start(s32[2,2,2,2]{3,2,1,0:T(2,128)S(1)} %constant_dynamic-update-slice_fusion.ids0_ref), channel_id=1, source_target_pairs={{0,64},{64,0},{1,65},{65,1},{2,66},{66,2},{3,67},{67,3},{4,68},{68... | collective-permute-start | bytes 200 | tf_op jit(solution)/shard_map/ppermute | solution.py:422
  18.6 8.0 %collective-permute-start.2 = (s32[2,2,2,2]{3,2,1,0:T(2,128)S(1)}, s32[2,2,2,2]{3,2,1,0:T(2,128)S(1)}, u32[]{:S(2)}, u32[]{:S(2)}) collective-permute-start(s32[2,2,2,2]{3,2,1,0:T(2,128)S(1)} %constant_dynamic-update-slice_fusion.ids0_ref), channel_id=1, source_target_pairs={{0,128},{128,0},{1,129},{129,1},{2,130},{130,2},{3,131},{131,3},{4... | collective-permute-start | bytes 200 | tf_op jit(solution)/shard_map/ppermute | solution.py:421
  20.1 6.5 %collective-permute-start.3 = (s32[2,2,2,2]{3,2,1,0:T(2,128)S(1)}, s32[2,2,2,2]{3,2,1,0:T(2,128)S(1)}, u32[]{:S(2)}, u32[]{:S(2)}) collective-permute-start(s32[2,2,2,2]{3,2,1,0:T(2,128)S(1)} %constant_dynamic-update-slice_fusion.ids0_ref), channel_id=1, source_target_pairs={{0,192},{64,128},{128,64},{192,0},{1,193},{65,129},{129,65},{193,1... | collective-permute-start | bytes 200 | tf_op jit(solution)/shard_map/ppermute | solution.py:423
  26.6 1.5 %collective-permute-start.6 = (bf16[128,1024]{1,0:T(8,128)(2,1)S(1)}, bf16[128,1024]{1,0:T(8,128)(2,1)S(1)}, u32[]{:S(2)}, u32[]{:S(2)}) collective-permute-start(bf16[128,1024]{1,0:T(8,128)(2,1)S(1)} %collective-permute-done.1.q0_ref), channel_id=1, source_target_pairs={{0,64},{64,0},{1,65},{65,1},{2,66},{66,2},{3,67},{67,3},{4,68},{68... | collective-permute-start | bytes 786440 | tf_op jit(solution)/shard_map/ppermute | solution.py:430
  26.7 5.4 %collective-permute-start.7 = (bf16[1056,128]{1,0:T(8,128)(2,1)S(1)}, bf16[1056,128]{1,0:T(8,128)(2,1)S(1)}, u32[]{:S(2)}, u32[]{:S(2)}) collective-permute-start(bf16[1056,128]{1,0:T(8,128)(2,1)S(1)} %get-tuple-element.37), channel_id=1, source_target_pairs={{0,64},{64,0},{1,65},{65,1},{2,66},{66,2},{3,67},{67,3},{4,68},{68... | collective-permute-start | bytes 811016 | tf_op jit(solution)/shard_map/ppermute | solution.py:434
  32.1 14.8 %collective-permute-start.10 = (bf16[1056,128]{1,0:T(8,128)(2,1)S(1)}, bf16[1056,128]{1,0:T(8,128)(2,1)S(1)}, u32[]{:S(2)}, u32[]{:S(2)}) collective-permute-start(bf16[1056,128]{1,0:T(8,128)(2,1)S(1)} %get-tuple-element.39), channel_id=1, source_target_pairs={{0,64},{64,0},{1,65},{65,1},{2,66},{66,2},{3,67},{67,3},{4,68},{68... | collective-permute-start | bytes 811016 | tf_op jit(solution)/shard_map/ppermute | solution.py:435
  40.4 10.7 %collective-permute-start.8 = (bf16[4,2,128,128]{3,2,1,0:T(8,128)(2,1)}, bf16[4,2,128,128]{3,2,1,0:T(8,128)(2,1)S(1)}, u32[]{:S(2)}, u32[]{:S(2)}) collective-permute-start(bf16[4,2,128,128]{3,2,1,0:T(8,128)(2,1)} %get-tuple-element.56), channel_id=1, source_target_pairs={{0,2},{2,4},{4,6},{6,0},{1,3},{3,5},{5,7},{7,1},{8,10},{10,12},{12... | collective-permute-start | bytes 786440 | tf_op jit(solution)/shard_map/ppermute | solution.py:440
  40.4 10.7 %collective-permute-start.9 = (bf16[4,2,128,128]{3,2,1,0:T(8,128)(2,1)}, bf16[4,2,128,128]{3,2,1,0:T(8,128)(2,1)S(1)}, u32[]{:S(2)}, u32[]{:S(2)}) collective-permute-start(bf16[4,2,128,128]{3,2,1,0:T(8,128)(2,1)} %get-tuple-element.55), channel_id=1, source_target_pairs={{0,6},{2,0},{4,2},{6,4},{1,7},{3,1},{5,3},{7,5},{8,14},{10,8},{12,... | collective-permute-start | bytes 786440 | tf_op jit(solution)/shard_map/ppermute | solution.py:441
  43.6 13.0 %collective-permute-start.13 = (bf16[4,2,128,128]{3,2,1,0:T(8,128)(2,1)}, bf16[4,2,128,128]{3,2,1,0:T(8,128)(2,1)S(1)}, u32[]{:S(2)}, u32[]{:S(2)}) collective-permute-start(bf16[4,2,128,128]{3,2,1,0:T(8,128)(2,1)} %get-tuple-element.55), channel_id=1, source_target_pairs={{0,2},{2,4},{4,6},{6,0},{1,3},{3,5},{5,7},{7,1},{8,10},{10,12},{12... | collective-permute-start | bytes 786440 | tf_op jit(solution)/shard_map/ppermute | solution.py:442
  43.6 13.0 %collective-permute-start.14 = (bf16[4,2,128,128]{3,2,1,0:T(8,128)(2,1)}, bf16[4,2,128,128]{3,2,1,0:T(8,128)(2,1)}, u32[]{:S(2)}, u32[]{:S(2)}) collective-permute-start(bf16[4,2,128,128]{3,2,1,0:T(8,128)(2,1)} %get-tuple-element.56), channel_id=1, source_target_pairs={{0,6},{2,0},{4,2},{6,4},{1,7},{3,1},{5,3},{7,5},{8,14},{10,8},{12,... | collective-permute-start | bytes 786440 | tf_op jit(solution)/shard_map/ppermute | solution.py:443
  47.0 14.0 %collective-permute-start.15 = (bf16[1056,128]{1,0:T(8,128)(2,1)S(1)}, bf16[1056,128]{1,0:T(8,128)(2,1)S(1)}, u32[]{:S(2)}, u32[]{:S(2)}) collective-permute-start(bf16[1056,128]{1,0:T(8,128)(2,1)S(1)} %merge.1), channel_id=1, source_target_pairs={{0,128},{128,0},{1,129},{129,1},{2,130},{130,2},{3,131},{131,3},{4... | collective-permute-start | bytes 811016 | tf_op jit(solution)/shard_map/ppermute | solution.py:451
  51.1 9.9 %collective-permute-start.11 = (bf16[4,2,128,128]{3,2,1,0:T(8,128)(2,1)S(1)}, bf16[4,2,128,128]{3,2,1,0:T(8,128)(2,1)S(1)}, u32[]{:S(2)}, u32[]{:S(2)}) collective-permute-start(bf16[4,2,128,128]{3,2,1,0:T(8,128)(2,1)S(1)} %collective-permute-done.8.refs_0_), channel_id=1, source_target_pairs={{0,2},{2,4},{4,6},{6,0},{1,3},{3,5},{5,7},{7,1},{8,10},{10,12},{12... | collective-permute-start | bytes 786440 | tf_op jit(solution)/shard_map/ppermute | solution.py:449
  51.1 9.9 %collective-permute-start.12 = (bf16[4,2,128,128]{3,2,1,0:T(8,128)(2,1)S(1)}, bf16[4,2,128,128]{3,2,1,0:T(8,128)(2,1)S(1)}, u32[]{:S(2)}, u32[]{:S(2)}) collective-permute-start(bf16[4,2,128,128]{3,2,1,0:T(8,128)(2,1)S(1)} %collective-permute-done.9.refs_3_), channel_id=1, source_target_pairs={{0,6},{2,0},{4,2},{6,4},{1,7},{3,1},{5,3},{7,5},{8,14},{10,8},{12,... | collective-permute-start | bytes 786440 | tf_op jit(solution)/shard_map/ppermute | solution.py:450
  63.5 13.8 %all-to-all-start.1 = ((bf16[8,128,128]{2,1,0:T(8,128)(2,1)}), bf16[8,128,128]{2,1,0:T(8,128)(2,1)S(1)}, u32[]{:S(2)}, u32[]{:S(2)}) async-start(bf16[8,128,128]{2,1,0:T(8,128)(2,1)} %attend_far.1.after_ref), calls=%async_computation.1 | async-start | bytes 524288 | tf_op jit(solution)/shard_map/all_to_all | solution.py:462
  78.1 10.0 %collective-permute-start.16 = (bf16[128,1024]{1,0:T(8,128)(2,1)S(1)}, bf16[128,1024]{1,0:T(8,128)(2,1)S(1)}, u32[]{:S(2)}, u32[]{:S(2)}) collective-permute-start(bf16[128,1024]{1,0:T(8,128)(2,1)S(1)} %convolution_convert_fusion), channel_id=1, source_target_pairs={{0,1},{1,0},{2,3},{3,2},{4,5},{5,4},{6,7},{7,6},{8,9},{9,8},{10,11... | collective-permute-start | bytes 786440 | tf_op jit(solution)/shard_map/ppermute | solution.py:472
  82.4 8.5 %collective-permute-start.17 = (bf16[128,1024]{1,0:T(8,128)(2,1)S(1)}, bf16[128,1024]{1,0:T(8,128)(2,1)S(1)}, u32[]{:S(2)}, u32[]{:S(2)}) collective-permute-start(bf16[128,1024]{1,0:T(8,128)(2,1)S(1)} %fusion.12), channel_id=1, source_target_pairs={{0,1},{1,0},{2,3},{3,2},{4,5},{5,4},{6,7},{7,6},{8,9},{9,8},{10,11... | collective-permute-start | bytes 786440 | tf_op jit(solution)/shard_map/ppermute | solution.py:472
